TPU v7x, 128 devices: a whole 4x4x4 slice. The times are simulated.
128 devices in a mesh: slab: 32 (over x, y, core), tile: 4 (over z).
Axes of the slice: x: 4, y: 4, z: 4, core: 2. Of those that a mesh axis runs over, the one named last changes fastest.
Arguments:
- frames: bfloat16 [128, 64, 256, 128], P('slab', 'tile'), may hold values from -21 to 21
- clip_frames: int32 [16], replicated, may hold values from 1 to 49, 128 in all
- norm_gain: float32 [128], replicated, may hold values from 0.1 to 1.9
- norm_bias: float32 [128], replicated, may hold values from -3 to 3
- conv_weight: bfloat16 [3, 3, 3, 128, 128], replicated, may hold values from -0.109375 to 0.109375
- conv_bias: float32 [128], replicated, may hold values from -3 to 3
- down_weight: bfloat16 [3, 3, 128, 128], replicated, may hold values from -0.1875 to 0.1875
- down_bias: float32 [128], replicated, may hold values from -3 to 3
Outputs:
- latent: bfloat16 [128, 32, 128, 128], P('slab', 'tile')
Inputs may be any that keep to these rules, and one draw needn't show every extreme that they name: `clip_frames`: frame counts of the 16 clips of the pack, in frame order; they sum to 128.
All inputs are finite; a program needn't handle non-finite values.
Results may differ from a plain program's by a relative error of at most 0.005.
Values may be sent and summed in bfloat16 or wider, within the bound.
No kernel may reach another device: no remote copies, remote signals or barrier semaphores. Data moves between devices by JAX's collectives and lax.ppermute only.
A program may use at most 128 MiB of HBM per device.

v0:
```python
import functools

import jax
import jax.numpy as jnp
from jax import lax
from jax.experimental import pallas as pl
from jax.experimental.pallas import tpu as pltpu
from jax.sharding import PartitionSpec as P

GROUPS = 32
EPSILON = 1e-06
VMEM_LIMIT = 60 * 1024 * 1024
HIGHEST = lax.Precision.HIGHEST
F32 = jnp.float32
BF16 = jnp.bfloat16


def sums_kernel(steps, x_ref, out_ref, acc):
    frame, part = pl.program_id(0), pl.program_id(1)
    rows, cols, chans = x_ref.shape[1:]
    x = x_ref[0].reshape(rows * cols // 64, 64, chans).astype(F32)
    one = jnp.sum(x, axis=0)
    two = jnp.sum(x * x, axis=0)

    @pl.when(part == 0)
    def _():
        acc[frame, 0] = one
        acc[frame, 1] = two

    @pl.when(part > 0)
    def _():
        acc[frame, 0] += one
        acc[frame, 1] += two

    @pl.when((frame == pl.num_programs(0) - 1) & (part == steps - 1))
    def _():
        both = [
            jnp.concatenate([jnp.sum(acc[f, i], axis=0, keepdims=True) for f in range(4)], axis=1)
            for i in range(2)
        ]
        row = lax.broadcasted_iota(jnp.int32, (4 * chans, chans), 0)
        lane = lax.broadcasted_iota(jnp.int32, (4 * chans, chans), 1)
        member = ((row >> 2) == lane).astype(F32)
        sums = jnp.dot(jnp.concatenate(both, axis=0), member, precision=HIGHEST, preferred_element_type=F32)
        out_ref[...] = jnp.broadcast_to(sums[None], out_ref.shape)


def frame_sums(frames, devices):
    count, rows, cols, chans = frames.shape
    steps = 2
    return pl.pallas_call(
        functools.partial(sums_kernel, steps),
        grid=(count, steps),
        in_specs=[pl.BlockSpec((1, rows // steps, cols, chans), lambda f, p: (f, p, 0, 0))],
        out_specs=pl.BlockSpec((devices, 2, chans), lambda f, p: (0, 0, 0)),
        out_shape=jax.ShapeDtypeStruct((devices, 2, chans), F32),
        scratch_shapes=[pltpu.VMEM((count, 2, 64, chans), F32)],
        compiler_params=pltpu.CompilerParams(vmem_limit_bytes=VMEM_LIMIT),
        name="frame_sums",
    )(frames)


def own_rows(step):
    if step == 0:
        return 0, 3
    if step < 7:
        return 2 * step + 1, 2
    return 15, 1


def block_kernel(
    cfg, pos_ref, clips_ref, sums_ref, gain_ref, bias_ref, w_ref, cb_ref, dw_ref, db_ref,
    early, late, top_early, top_late, bot_early, bot_late, *rest,
):
    base, e0, l0, o0, aliased = cfg
    if aliased:
        rest = rest[1:]
    out_ref, xin, xs, wa, wbe, wbo, wd, vsum, obuf, sems, osems = rest[:11]
    act = rest[11:30]
    res = rest[30:47]
    mix = rest[47:64]
    count = 4
    slab, tile, tiles = pos_ref[0], pos_ref[1], pos_ref[2]

    copies = {}
    used = [0]

    def start(step, src, dst):
        copy = pltpu.make_async_copy(src, dst, sems.at[used[0]])
        used[0] += 1
        copy.start()
        copies.setdefault(step, []).append(copy)

    for s in range(9):
        if s == 0:
            for src, b, slot in ((top_early, e0, 0), (top_late, l0, 2)):
                start(0, src.at[pl.ds(b, 2), pl.ds(0, 1)], xin.at[pl.ds(slot, 2), pl.ds(0, 1)])
        if s < 8:
            lo, n = own_rows(s)
            for src, b, slot in ((early, e0, 0), (late, l0, 2)):
                start(s, src.at[pl.ds(b, 2), pl.ds(lo, n)], xin.at[pl.ds(slot, 2), pl.ds(lo + 1, n)])
        if s >= 7:
            for src, b, slot in ((bot_early, e0, 0), (bot_late, l0, 2)):
                start(s, src.at[pl.ds(b, 2), pl.ds(s - 7, 1)], xin.at[pl.ds(slot, 2), pl.ds(s + 10, 1)])

    first = slab * count + base
    starts = [jnp.int32(0)] * 4
    ends = [jnp.int32(1)] * 4
    begin = jnp.int32(0)
    for c in range(clips_ref.shape[0]):
        end = begin + clips_ref[c]
        for f in range(4):
            inside = (begin <= first + f) & (first + f < end)
            starts[f] = jnp.where(inside, begin, starts[f])
            ends[f] = jnp.where(inside, end, ends[f])
        begin = end
    source = [[jnp.maximum(first + t + k - 2, starts[t]) - first for k in range(3)] for t in (2, 3)]

    slabs = sums_ref.shape[0] // 4
    sums = jnp.sum(sums_ref[...].reshape(slabs, 4, 2, 128), axis=1)
    frame_of = 4 * lax.broadcasted_iota(jnp.int32, (slabs, 2, 128), 0) + (
        lax.broadcasted_iota(jnp.int32, (slabs, 2, 128), 2) >> 5
    )
    for f in range(4):
        inside = (frame_of >= starts[f]) & (frame_of < ends[f])
        vsum[2 * f:2 * f + 2, :] = jnp.sum(jnp.where(inside, sums, 0.0), axis=0)
    group = lax.broadcasted_iota(jnp.int32, (128, 128), 0) & (GROUPS - 1)
    chan = lax.broadcasted_iota(jnp.int32, (128, 128), 1) >> 2
    totals = jnp.dot(vsum[...], (group == chan).astype(F32), precision=HIGHEST, preferred_element_type=F32)
    half_scale, half_shift = [], []
    for f in range(4):
        pixels = (ends[f] - starts[f]) * (tiles * 16 * 256 * 4)
        number = jnp.full((1, 128), pixels, jnp.int32).astype(F32)
        mean = totals[2 * f:2 * f + 1] / number
        variance = totals[2 * f + 1:2 * f + 2] / number - mean * mean
        scale = gain_ref[...] * lax.rsqrt(variance + EPSILON)
        half_scale.append(0.5 * scale)
        half_shift.append(0.5 * (bias_ref[...] - mean * scale))

    zero = jnp.zeros((128, 128), BF16)
    for k in range(3):
        for dy in range(3):
            w0, w1, w2 = (w_ref[k, dy, dx] for dx in range(3))
            r = (dy * 3 + k) * 256
            wa[r:r + 128, 0:128] = w1
            wa[r:r + 128, 128:256] = w0
            wa[r + 128:r + 256, 0:128] = w2
            wa[r + 128:r + 256, 128:256] = w1
            for wb, w in ((wbe, w0), (wbo, w2)):
                a = (dy * 3 + k) * 128
                b = ((dy + 1) * 3 + k) * 128
                wb[a:a + 128, 0:128] = w
                wb[b:b + 128, 128:256] = w
        for wb in (wbe, wbo):
            wb[k * 128:(k + 1) * 128, 128:256] = zero
            wb[(9 + k) * 128:(10 + k) * 128, 0:128] = zero
    for dy in range(3):
        r = dy * 256
        wd[r:r + 128, 0:128] = dw_ref[dy, 0]
        wd[r + 128:r + 256, 0:128] = dw_ref[dy, 1]
        wd[r:r + 128, 128:256] = dw_ref[dy, 2]
        wd[r + 128:r + 256, 128:256] = zero

    def activate(idx, f, slot):
        xs[slot] = xin[f, idx].astype(F32)
        for p in range(2):
            lanes = slice(p * 128, (p + 1) * 128)
            v = xs[slot, pl.ds(p, 128, stride=2), :]
            if f >= 2 and 1 <= idx <= 17:
                res[idx - 1][f - 2, :, lanes] = v.astype(BF16)
            u = v * half_scale[f] + half_shift[f]
            a = u + u * jnp.tanh(u)
            if idx == 0:
                a = jnp.where(tile == 0, 0.0, a)
            if idx >= 17:
                a = jnp.where(tile == tiles - 1, 0.0, a)
            act[idx][f, :, lanes] = a.astype(BF16)

    def act_step(s):
        if s > 8:
            return
        for copy in copies[s]:
            copy.wait()
        rows = [0, 1, 2, 3] if s == 0 else ([2 * s + 2, 2 * s + 3] if s < 8 else [18])
        for i, idx in enumerate(rows):
            for f in range(4):
                activate(idx, f, (s % 2) * 16 + i * 4 + f)

    pair = lax.broadcasted_iota(jnp.int32, (128, 128), 0)

    def from_before(p):
        return jnp.where(pair == 0, 0.0, pltpu.roll(p, 1, 0))

    def from_after(p):
        return jnp.where(pair == 127, 0.0, pltpu.roll(p, 127, 0))

    cb = jnp.concatenate([cb_ref[...], cb_ref[...]], axis=1)

    def dot(a, b):
        return jnp.dot(a, b, preferred_element_type=F32)

    def finish(y, t, own, even, odd):
        m = res[y][t].astype(F32) + cb + own
        for p, v in ((0, m[:, :128] + from_before(even)), (1, m[:, 128:] + from_after(odd))):
            if y == 16:
                v = jnp.where(tile == tiles - 1, 0.0, v)
            mix[y][t, :, p * 128:(p + 1) * 128] = v.astype(BF16)

    def conv_step(s):
        y = 2 * s
        n = 1 if s == 8 else 2
        blocks = []
        for t in range(2):
            for i in range(n):
                blocks.append(jnp.concatenate(
                    [act[y + i + dy][source[t][k]] for dy in range(3) for k in range(3)], axis=1))
        own = dot(jnp.concatenate(blocks, axis=0), wa[...])
        sides = []
        for p, wb in ((1, wbe), (0, wbo)):
            left = jnp.concatenate([
                jnp.concatenate(
                    [act[y + q][source[t][k], :, p * 128:(p + 1) * 128] for q in range(n + 2) for k in range(3)],
                    axis=1)
                for t in range(2)], axis=0)
            sides.append(dot(left, wb[...] if n == 2 else wb[0:1152, 0:128]))
        for t in range(2):
            for i in range(n):
                m = (t * n + i) * 128
                even, odd = (v[t * 128:(t + 1) * 128, i * 128:(i + 1) * 128] for v in sides)
                finish(y + i, t, own[m:m + 128], even, odd)

    outs = []

    def out_row(r):
        left = jnp.concatenate(
            [jnp.concatenate([mix[2 * r + dy][t] for dy in range(3)], axis=1) for t in range(2)], axis=0)
        p = dot(left, wd[...])
        for t in range(2):
            q = p[t * 128:(t + 1) * 128]
            obuf[r, t, 0] = (q[:, :128] + from_after(q[:, 128:]) + db_ref[...]).astype(BF16)
        copy = pltpu.make_async_copy(obuf.at[r], out_ref.at[pl.ds(o0, 2), pl.ds(r, 1)], osems.at[r])
        copy.start()
        outs.append(copy)

    act_step(0)
    for s in range(9):
        conv_step(s)
        act_step(s + 1)
        if s >= 1:
            out_row(s - 1)
    for copy in outs:
        copy.wait()


def two_frames(cfg, small, big, before=None):
    anywhere = pl.BlockSpec(memory_space=pl.ANY)
    vmem = pl.BlockSpec(memory_space=pltpu.VMEM)
    smem = pl.BlockSpec(memory_space=pltpu.SMEM)
    scratch = [
        pltpu.VMEM((4, 19, 256, 128), BF16),
        pltpu.VMEM((32, 256, 128), F32),
        pltpu.VMEM((2304, 256), BF16),
        pltpu.VMEM((1536, 256), BF16),
        pltpu.VMEM((1536, 256), BF16),
        pltpu.VMEM((768, 256), BF16),
        pltpu.VMEM((8, 128), F32),
        pltpu.VMEM((8, 2, 1, 128, 128), BF16),
        pltpu.SemaphoreType.DMA((22,)),
        pltpu.SemaphoreType.DMA((8,)),
    ]
    scratch += [pltpu.VMEM((4, 128, 256), BF16)] * 19
    scratch += [pltpu.VMEM((2, 128, 256), BF16)] * 34
    operands = list(small) + list(big)
    specs = [smem, smem] + [vmem] * 7 + [anywhere] * 6
    aliases = {}
    if before is not None:
        aliases = {len(operands): 0}
        operands.append(before)
        specs.append(anywhere)
    return pl.pallas_call(
        functools.partial(block_kernel, cfg + (before is not None,)),
        out_shape=jax.ShapeDtypeStruct((4, 8, 128, 128), BF16),
        in_specs=specs,
        out_specs=anywhere,
        scratch_shapes=scratch,
        input_output_aliases=aliases,
        compiler_params=pltpu.CompilerParams(vmem_limit_bytes=VMEM_LIMIT),
        cost_estimate=pl.CostEstimate(flops=16 * 10**9, bytes_accessed=6 * 2**20, transcendentals=10**7),
        name="two_frames",
    )(*operands)


def shards(frames, clip_frames, norm_gain, norm_bias, conv_weight, conv_bias, down_weight, down_bias):
    slabs, tiles = lax.axis_size("slab"), lax.axis_size("tile")
    both = ("slab", "tile")

    def flat(s, t):
        return s * tiles + t

    earlier = lax.ppermute(frames[2:4], "slab", [(s, s + 1) for s in range(slabs - 1)])
    top = lax.ppermute(frames[:, 15:16], "tile", [(t, t + 1) for t in range(tiles - 1)])
    bottom = lax.ppermute(frames[:, 0:2], "tile", [(t + 1, t) for t in range(tiles - 1)])
    cells = [(s, t) for s in range(slabs - 1) for t in range(tiles - 1)]
    top_earlier = lax.ppermute(frames[2:4, 15:16], both, [(flat(s, t), flat(s + 1, t + 1)) for s, t in cells])
    bottom_earlier = lax.ppermute(frames[2:4, 0:2], both, [(flat(s, t + 1), flat(s + 1, t)) for s, t in cells])

    sums = lax.all_to_all(frame_sums(frames, slabs * tiles), both, 0, 0)
    place = jnp.stack([lax.axis_index("slab"), lax.axis_index("tile"), jnp.int32(tiles)]).astype(jnp.int32)
    small = (
        place, clip_frames, sums, norm_gain[None], norm_bias[None], conv_weight, conv_bias[None], down_weight,
        down_bias[None],
    )
    last = two_frames((0, 0, 2, 2), small, (frames, frames, top, top, bottom, bottom))
    return two_frames(
        (-2, 0, 0, 0), small, (earlier, frames, top_earlier, top, bottom_earlier, bottom), before=last)


def solution(mesh):
    return jax.shard_map(
        shards,
        mesh=mesh,
        in_specs=(P("slab", "tile", None, None), P(), P(), P(), P(), P(), P(), P()),
        out_specs=P("slab", "tile", None, None),
        check_vma=False,
    )
```

profile of v0, /device:TPU:1, one launch (start us, length us, event | category | flops | bytes accessed | tf_op | source)
XLA Modules:
  0.0 77.5 jit_solution(3106852993267593871)
XLA Ops:
  0.0 1.8 %slice.15 = bf16[2,16,256,128]{3,2,1,0:T(8,128)(2,1)S(1)} slice(bf16[4,16,256,128]{3,2,1,0:T(8,128)(2,1)} %late.3), slice={[2:4], [0:16], [0:256], [0:128]} | slice | bytes 4194304 | tf_op jit(solution)/shard_map/slice | solution.py:300
  1.8 4.6 %collective-permute-start = (bf16[2,16,256,128]{3,2,1,0:T(8,128)(2,1)S(1)}, bf16[2,16,256,128]{3,2,1,0:T(8,128)(2,1)}, u32[]{:S(2)}, u32[]{:S(2)}) collective-permute-start(bf16[2,16,256,128]{3,2,1,0:T(8,128)(2,1)S(1)} %slice.15), channel_id=1, source_target_pairs={{0,4},{4,8},{8,12},{12,16},{16,20},{20,24},{24,28},{28,32},{32,36}... | collective-permute-start | bytes 6291464 | tf_op jit(solution)/shard_map/ppermute | solution.py:300
  6.4 1.1 %slice.19 = bf16[4,2,256,128]{3,2,1,0:T(8,128)(2,1)S(1)} slice(bf16[4,16,256,128]{3,2,1,0:T(8,128)(2,1)} %late.3), slice={[0:4], [0:2], [0:256], [0:128]} | slice | bytes 1048576 | tf_op jit(solution)/shard_map/slice | solution.py:302
  7.5 1.3 %collective-permute-start.4 = (bf16[4,2,256,128]{3,2,1,0:T(8,128)(2,1)S(1)}, bf16[4,2,256,128]{3,2,1,0:T(8,128)(2,1)}, u32[]{:S(2)}, u32[]{:S(2)}) collective-permute-start(bf16[4,2,256,128]{3,2,1,0:T(8,128)(2,1)S(1)} %slice.19), channel_id=1, source_target_pairs={{1,0},{2,1},{3,2},{5,4},{6,5},{7,6},{9,8},{10,9},{11,10},{13,12},{... | collective-permute-start | bytes 1572872 | tf_op jit(solution)/shard_map/ppermute | solution.py:302
  8.8 1.0 %slice.17 = bf16[4,1,256,128]{3,2,1,0:T(8,128)(2,1)S(1)} slice(bf16[4,16,256,128]{3,2,1,0:T(8,128)(2,1)} %late.3), slice={[0:4], [15:16], [0:256], [0:128]} | slice | bytes 524288 | tf_op jit(solution)/shard_map/slice | solution.py:301
  9.8 4.9 %collective-permute-start.2 = (bf16[4,1,256,128]{3,2,1,0:T(8,128)(2,1)S(1)}, bf16[4,1,256,128]{3,2,1,0:T(8,128)(2,1)}, u32[]{:S(2)}, u32[]{:S(2)}) collective-permute-start(bf16[4,1,256,128]{3,2,1,0:T(8,128)(2,1)S(1)} %slice.17), channel_id=1, source_target_pairs={{0,1},{1,2},{2,3},{4,5},{5,6},{6,7},{8,9},{9,10},{10,11},{12,13},{... | collective-permute-start | bytes 786440 | tf_op jit(solution)/shard_map/ppermute | solution.py:301
  14.7 5.8 %frame_sums.1 = f32[128,2,128]{2,1,0:T(2,128)} custom-call(bf16[4,16,256,128]{3,2,1,0:T(8,128)(2,1)} %late.3), custom_call_target="tpu_custom_call" | custom-call | tf_op jit(solution)/shard_map/frame_sums/pallas_call | solution.py:51
  20.5 9.6 %all-to-all-start = ((f32[128,2,128]{2,1,0:T(2,128)}), f32[128,2,128]{2,1,0:T(2,128)S(1)}, u32[]{:S(2)}, u32[]{:S(2)}) async-start(f32[128,2,128]{2,1,0:T(2,128)} %frame_sums.1), calls=%async_computation | async-start | bytes 262144 | tf_op jit(solution)/shard_map/all_to_all | solution.py:307
  30.1 0.9 %slice.16 = bf16[2,1,256,128]{3,2,1,0:T(8,128)(2,1)S(1)} slice(bf16[4,16,256,128]{3,2,1,0:T(8,128)(2,1)} %late.3), slice={[2:4], [15:16], [0:256], [0:128]} | slice | bytes 262144 | tf_op jit(solution)/shard_map/slice | solution.py:304
  31.0 4.6 %collective-permute-start.1 = (bf16[2,1,256,128]{3,2,1,0:T(8,128)(2,1)S(1)}, bf16[2,1,256,128]{3,2,1,0:T(8,128)(2,1)S(1)}, u32[]{:S(2)}, u32[]{:S(2)}) collective-permute-start(bf16[2,1,256,128]{3,2,1,0:T(8,128)(2,1)S(1)} %slice.16), channel_id=1, source_target_pairs={{0,5},{1,6},{2,7},{4,9},{5,10},{6,11},{8,13},{9,14},{10,15},{12,17... | collective-permute-start | bytes 393224 | tf_op jit(solution)/shard_map/ppermute | solution.py:304
  35.7 1.0 %slice.18 = bf16[2,2,256,128]{3,2,1,0:T(8,128)(2,1)S(1)} slice(bf16[4,16,256,128]{3,2,1,0:T(8,128)(2,1)} %late.3), slice={[2:4], [0:2], [0:256], [0:128]} | slice | bytes 524288 | tf_op jit(solution)/shard_map/slice | solution.py:305
  36.6 1.3 %collective-permute-start.3 = (bf16[2,2,256,128]{3,2,1,0:T(8,128)(2,1)S(1)}, bf16[2,2,256,128]{3,2,1,0:T(8,128)(2,1)}, u32[]{:S(2)}, u32[]{:S(2)}) collective-permute-start(bf16[2,2,256,128]{3,2,1,0:T(8,128)(2,1)S(1)} %slice.18), channel_id=1, source_target_pairs={{1,4},{2,5},{3,6},{5,8},{6,9},{7,10},{9,12},{10,13},{11,14},{13,16... | collective-permute-start | bytes 786440 | tf_op jit(solution)/shard_map/ppermute | solution.py:305
  38.0 0.6 pad_add_fusion.pos_ref
  38.5 1.5 %all-to-all-done.sums_ref = f32[128,2,128]{2,1,0:T(2,128)S(1)} async-done(((f32[128,2,128]{2,1,0:T(2,128)}), f32[128,2,128]{2,1,0:T(2,128)S(1)}, u32[]{:S(2)}, u32[]{:S(2)}) %all-to-all-start) | async-done | bytes 131104 | tf_op jit(solution)/shard_map/all_to_all | solution.py:307
  40.0 0.0 copy-start
  40.0 0.0 collective-permute-done.2.top_early.top_late
  40.0 0.0 collective-permute-done.4.bot_early.bot_late
  40.0 0.6 copy-done
  40.6 18.0 %two_frames.2.rest_0_ = bf16[4,8,128,128]{3,2,1,0:T(8,128)(2,1)} custom-call(s32[3]{0:T(128)} %pad_add_fusion.pos_ref, s32[16]{0:T(128)} %clips_ref.3, f32[128,2,128]{2,1,0:T(2,128)} %copy-done, f32[1,128]{1,0:T(1,128)} %bitcast.6, f32[1,128]{1,0:T(1,128)} %bitcast.8, bf16[3,3,3,128,128]{4,3,2,1,0:T(8,128)(2,1)} %w_ref.3, f32[1,128]{1,0:T(1,128)} %bitcast.10, ...), custom_call_target="tpu_custom_call" | custom-call | flops 16000000000 | bytes 6291456 | tf_op jit(solution)/shard_map/two_frames/pallas_call | solution.py:280
  58.6 0.0 collective-permute-done.1.top_early
  58.6 0.0 copy-start.1
  58.6 0.0 collective-permute-done.3.bot_early
  58.7 0.0 collective-permute-done.early
  58.7 0.6 copy-done.1
  59.3 18.0 %two_frames.3 = bf16[4,8,128,128]{3,2,1,0:T(8,128)(2,1)} custom-call(s32[3]{0:T(128)} %pad_add_fusion.pos_ref, s32[16]{0:T(128)} %clips_ref.3, f32[128,2,128]{2,1,0:T(2,128)} %copy-done, f32[1,128]{1,0:T(1,128)} %bitcast.7, f32[1,128]{1,0:T(1,128)} %bitcast.9, bf16[3,3,3,128,128]{4,3,2,1,0:T(8,128)(2,1)} %w_ref.3, ...), custom_call_target="tpu_custom_call", output_to_operand_aliasing={{}: (15, {})} | custom-call | flops 16000000000 | bytes 6291456 | tf_op jit(solution)/shard_map/two_frames/pallas_call | solution.py:280
Async XLA Ops:
  1.8 56.8 %collective-permute-start = (bf16[2,16,256,128]{3,2,1,0:T(8,128)(2,1)S(1)}, bf16[2,16,256,128]{3,2,1,0:T(8,128)(2,1)}, u32[]{:S(2)}, u32[]{:S(2)}) collective-permute-start(bf16[2,16,256,128]{3,2,1,0:T(8,128)(2,1)S(1)} %slice.15), channel_id=1, source_target_pairs={{0,4},{4,8},{8,12},{12,16},{16,20},{20,24},{24,28},{28,32},{32,36}... | collective-permute-start | bytes 6291464 | tf_op jit(solution)/shard_map/ppermute | solution.py:300
  7.5 32.5 %collective-permute-start.4 = (bf16[4,2,256,128]{3,2,1,0:T(8,128)(2,1)S(1)}, bf16[4,2,256,128]{3,2,1,0:T(8,128)(2,1)}, u32[]{:S(2)}, u32[]{:S(2)}) collective-permute-start(bf16[4,2,256,128]{3,2,1,0:T(8,128)(2,1)S(1)} %slice.19), channel_id=1, source_target_pairs={{1,0},{2,1},{3,2},{5,4},{6,5},{7,6},{9,8},{10,9},{11,10},{13,12},{... | collective-permute-start | bytes 1572872 | tf_op jit(solution)/shard_map/ppermute | solution.py:302
  9.8 30.2 %collective-permute-start.2 = (bf16[4,1,256,128]{3,2,1,0:T(8,128)(2,1)S(1)}, bf16[4,1,256,128]{3,2,1,0:T(8,128)(2,1)}, u32[]{:S(2)}, u32[]{:S(2)}) collective-permute-start(bf16[4,1,256,128]{3,2,1,0:T(8,128)(2,1)S(1)} %slice.17), channel_id=1, source_target_pairs={{0,1},{1,2},{2,3},{4,5},{5,6},{6,7},{8,9},{9,10},{10,11},{12,13},{... | collective-permute-start | bytes 786440 | tf_op jit(solution)/shard_map/ppermute | solution.py:301
  20.5 19.5 %all-to-all-start = ((f32[128,2,128]{2,1,0:T(2,128)}), f32[128,2,128]{2,1,0:T(2,128)S(1)}, u32[]{:S(2)}, u32[]{:S(2)}) async-start(f32[128,2,128]{2,1,0:T(2,128)} %frame_sums.1), calls=%async_computation | async-start | bytes 262144 | tf_op jit(solution)/shard_map/all_to_all | solution.py:307
  31.0 27.6 %collective-permute-start.1 = (bf16[2,1,256,128]{3,2,1,0:T(8,128)(2,1)S(1)}, bf16[2,1,256,128]{3,2,1,0:T(8,128)(2,1)S(1)}, u32[]{:S(2)}, u32[]{:S(2)}) collective-permute-start(bf16[2,1,256,128]{3,2,1,0:T(8,128)(2,1)S(1)} %slice.16), channel_id=1, source_target_pairs={{0,5},{1,6},{2,7},{4,9},{5,10},{6,11},{8,13},{9,14},{10,15},{12,17... | collective-permute-start | bytes 393224 | tf_op jit(solution)/shard_map/ppermute | solution.py:304
  36.6 22.0 %collective-permute-start.3 = (bf16[2,2,256,128]{3,2,1,0:T(8,128)(2,1)S(1)}, bf16[2,2,256,128]{3,2,1,0:T(8,128)(2,1)}, u32[]{:S(2)}, u32[]{:S(2)}) collective-permute-start(bf16[2,2,256,128]{3,2,1,0:T(8,128)(2,1)S(1)} %slice.18), channel_id=1, source_target_pairs={{1,4},{2,5},{3,6},{5,8},{6,9},{7,10},{9,12},{10,13},{11,14},{13,16... | collective-permute-start | bytes 786440 | tf_op jit(solution)/shard_map/ppermute | solution.py:305
  40.0 0.6 copy-start
  58.6 0.7 copy-start.1
where the time goes:
time: 78 us; the launch traced here: 77.5 us
  Pallas kernels  41.8 us (54%)
  starting transfers between devices  26.3 us (34%)
  local copies, waits for them, and re-layouts  7.04 us (9%)
  waiting for transfers between devices  1.47 us (2%)
    pallas_call x2, Pallas kernels, two_frames(): pl.pallas_call(functools.partial(block_kernel, cfg + (before is not None,...  36 us
    all_to_all x1, starting transfers between devices, shards(): sums = lax.all_to_all(frame_sums(frames, slabs * tiles), both, 0, 0)  9.59 us
    pallas_call x1, Pallas kernels, frame_sums(): pl.pallas_call(functools.partial(sums_kernel, steps), grid=(count, steps)...  5.84 us
    ppermute x1, starting transfers between devices, shards(): lax.ppermute(frames[:, 15:16], 'tile', [(t, t + 1) for t in range(tiles -...  4.88 us
    ppermute x1, starting transfers between devices, shards(): lax.ppermute(frames[2:4, 15:16], both, [(flat(s, t), flat(s + 1, t + 1))...  4.63 us
    ppermute x1, starting transfers between devices, shards(): lax.ppermute(frames[2:4], 'slab', [(s, s + 1) for s in range(slabs - 1)])  4.6 us
    slice x1, local copies, waits for them, and re-layouts, shards(): frames[2:4]  1.8 us
  transfers between devices with their start and end apart: 6, of which 1 were waited for; matrix products, arithmetic and copies ran while one was open for 6% of the time, Pallas kernels for 31%

commit v1 on v0

v1 whole, which is shorter than its diff:
```python
import functools

import jax
import jax.numpy as jnp
from jax import lax
from jax.experimental import pallas as pl
from jax.experimental.pallas import tpu as pltpu
from jax.sharding import PartitionSpec as P

GROUPS = 32
EPSILON = 1e-06
VMEM_LIMIT = 36 * 1024 * 1024
FLOPS = 200 * 10**9
F32 = jnp.float32
BF16 = jnp.bfloat16


def gathered(x, member):
    parts = []
    for _ in range(3):
        parts.append(x.astype(BF16))
        x = x - parts[-1].astype(F32)
    n = x.shape[0]
    out = jnp.dot(jnp.concatenate(parts, axis=0), member.astype(BF16), preferred_element_type=F32)
    return out[:n] + out[n:2 * n] + out[2 * n:]


def sums_kernel(pieces, x_ref, out_ref, far_ref, near_ref, top_ref, bottom_ref, corner_top_ref, corner_bottom_ref, xin, load, store):
    count, rows, cols, chans = x_ref.shape
    part = rows // pieces
    order = [2, 3, 0, 1]
    loads = {}
    for f in order:
        for p in range(pieces):
            cut = pl.ds(p * part, part)
            copy = pltpu.make_async_copy(x_ref.at[f, cut], xin.at[f, cut], load.at[f * pieces + p])
            copy.start()
            loads[f, p] = copy
    stores = []

    def send(src, dst):
        copy = pltpu.make_async_copy(src, dst, store.at[len(stores)])
        copy.start()
        stores.append(copy)

    sums = {}
    for f in order:
        one = two = jnp.zeros((32, chans), F32)
        for p in range(pieces):
            loads[f, p].wait()
            if p == pieces - 1:
                send(xin.at[f, pl.ds(0, 2)], bottom_ref.at[f])
                send(xin.at[f, pl.ds(rows - 1, 1)], top_ref.at[f])
                if f >= 2:
                    send(xin.at[f], (far_ref, near_ref)[f - 2].at[0])
                    send(xin.at[f, pl.ds(0, 2)], corner_bottom_ref.at[f - 2])
                    send(xin.at[f, pl.ds(rows - 1, 1)], corner_top_ref.at[f - 2])

            def row(i, both, f=f, p=p):
                x = xin[f, p * part + i].astype(F32).reshape(cols // 32, 32, chans)
                return both[0] + jnp.sum(x, axis=0), both[1] + jnp.sum(x * x, axis=0)

            one, two = lax.fori_loop(0, part, row, (one, two))
        sums[f] = [jnp.sum(v, axis=0, keepdims=True) for v in (one, two)]
    both = jnp.concatenate([jnp.concatenate([sums[f][i] for f in range(count)], axis=1) for i in range(2)], axis=0)
    row = lax.broadcasted_iota(jnp.int32, (4 * chans, chans), 0)
    lane = lax.broadcasted_iota(jnp.int32, (4 * chans, chans), 1)
    member = ((row >> 2) == lane).astype(F32)
    packed = gathered(both, member)
    out_ref[...] = jnp.broadcast_to(packed[None], out_ref.shape)
    for copy in stores:
        copy.wait()


def sums_and_rows(frames, devices):
    count, rows, cols, chans = frames.shape
    pieces = 4
    anywhere = pl.BlockSpec(memory_space=pl.ANY)
    shapes = [(1, rows), (1, rows), (count, 1), (count, 2), (2, 1), (2, 2)]
    return pl.pallas_call(
        functools.partial(sums_kernel, pieces),
        in_specs=[anywhere],
        out_specs=[pl.BlockSpec(memory_space=pltpu.VMEM)] + [anywhere] * 6,
        out_shape=[jax.ShapeDtypeStruct((devices, 2, chans), F32)]
        + [jax.ShapeDtypeStruct(s + (cols, chans), BF16) for s in shapes],
        scratch_shapes=[
            pltpu.VMEM((count, rows, cols, chans), BF16),
            pltpu.SemaphoreType.DMA((count * pieces,)),
            pltpu.SemaphoreType.DMA((14,)),
        ],
        compiler_params=pltpu.CompilerParams(vmem_limit_bytes=60 * 1024 * 1024),
        name="sums_and_rows",
    )(frames)


def block_kernel(
    base, target, groups, pos_ref, clips_ref, gain_ref, bias_ref, cb_ref, db_ref, sums_hbm, w_hbm, dw_hbm, *rest,
):
    inputs, rest = rest[:groups[0]], rest[groups[0]:]
    out_ref, xin, xs, wa, wbe, wbo, wd, vsum, obuf, sums_ref, w_ref, dw_ref, sems, osem = rest[:14]
    rows = rest[14:]
    act, res, mix = rows[:19], rows[19:36], rows[36:]
    count, slots = 2, 4
    slab, tile, tiles = pos_ref[0], pos_ref[1], pos_ref[2]

    copies = {}
    used = [0]

    def arrive(step):
        for copy in copies[step]:
            copy.wait()

    def start(step, src, dst):
        copy = pltpu.make_async_copy(src, dst, sems.at[used[0]])
        used[0] += 1
        copy.start()
        copies.setdefault(step, []).append(copy)

    def fetch(step, which, first_row, number, at):
        for slot, n, *places in groups[1]:
            ref, index = places[which]
            src = inputs[ref].at[pl.ds(index, n), pl.ds(first_row, number)]
            start(step, src, xin.at[pl.ds(slot, n), pl.ds(at, number)])

    start(0, sums_hbm, sums_ref)
    fetch(0, 1, 0, 1, 0)
    fetch(0, 0, 0, 3, 1)
    start(0, w_hbm, w_ref)
    start(0, dw_hbm, dw_ref)
    fetch(1, 0, 3, 13, 4)
    fetch(1, 2, 0, 2, 17)

    first = slab * 4 + base
    starts = [jnp.int32(0)] * slots
    ends = [jnp.int32(1)] * slots
    begin = jnp.int32(0)
    for c in range(clips_ref.shape[0]):
        end = begin + clips_ref[c]
        for f in range(slots):
            inside = (begin <= first + f) & (first + f < end)
            starts[f] = jnp.where(inside, begin, starts[f])
            ends[f] = jnp.where(inside, end, ends[f])
        begin = end
    opens = [starts[f] == first + f for f in range(slots)]
    second = [starts[f] == first + f - 1 for f in range(slots)]

    arrive(0)
    slabs = sums_ref.shape[0] // 4
    sums = jnp.sum(sums_ref[...].reshape(slabs, 4, 2, 128), axis=1)
    frame_of = 4 * lax.broadcasted_iota(jnp.int32, (slabs, 2, 128), 0) + (
        lax.broadcasted_iota(jnp.int32, (slabs, 2, 128), 2) >> 5
    )
    for f in range(slots):
        inside = (frame_of >= starts[f]) & (frame_of < ends[f])
        vsum[2 * f:2 * f + 2, :] = jnp.sum(jnp.where(inside, sums, 0.0), axis=0)
    group = lax.broadcasted_iota(jnp.int32, (128, 128), 0) & (GROUPS - 1)
    chan = lax.broadcasted_iota(jnp.int32, (128, 128), 1) >> 2
    totals = gathered(vsum[...], (group == chan).astype(F32))
    half_scale, half_shift = [], []
    for f in range(slots):
        pixels = (ends[f] - starts[f]) * (tiles * 16 * 256 * 4)
        number = jnp.full((1, 128), pixels, jnp.int32).astype(F32)
        mean = totals[2 * f:2 * f + 1] / number
        variance = totals[2 * f + 1:2 * f + 2] / number - mean * mean
        scale = gain_ref[...] * lax.rsqrt(variance + EPSILON)
        half_scale.append(0.5 * scale)
        half_shift.append(0.5 * (bias_ref[...] - mean * scale))

    def activate(idx, slot):
        for f in range(slots):
            xs[slot + f] = xin[f, idx].astype(F32)
        for p in range(2):
            lanes = slice(p * 128, (p + 1) * 128)
            planes = []
            for f in range(slots):
                v = xs[slot + f, pl.ds(p, 128, stride=2), :]
                if f >= 2 and 1 <= idx <= 17:
                    res[idx - 1][f - 2, :, lanes] = v.astype(BF16)
                u = v * half_scale[f] + half_shift[f]
                a = u + u * jnp.tanh(u)
                if idx == 0:
                    a = jnp.where(tile == 0, 0.0, a)
                if idx >= 17:
                    a = jnp.where(tile == tiles - 1, 0.0, a)
                planes.append(a.astype(BF16))
            for f in range(2, slots):
                now, before, oldest = planes[f], planes[f - 1], planes[f - 2]
                before = jnp.where(opens[f], now, before)
                oldest = jnp.where(opens[f] | second[f], before, oldest)
                for k, plane in enumerate((oldest, before, now)):
                    act[idx][3 * (f - 2) + k, :, lanes] = plane.astype(BF16)

    def act_step(s):
        rows = [0, 1, 2, 3] if s == 0 else ([2 * s + 2, 2 * s + 3] if s < 8 else [18])
        for i, idx in enumerate(rows):
            activate(idx, (s % 2) * 4 * slots + i * slots)

    def build_weights():
        zero = jnp.zeros((128, 128), BF16)
        for k in range(3):
            for dy in range(3):
                w0, w1, w2 = (w_ref[k, dy, dx] for dx in range(3))
                r = (dy * 3 + k) * 256
                wa[r:r + 128, 0:128] = w1
                wa[r:r + 128, 128:256] = w0
                wa[r + 128:r + 256, 0:128] = w2
                wa[r + 128:r + 256, 128:256] = w1
                for wb, w in ((wbe, w0), (wbo, w2)):
                    a = (dy * 3 + k) * 128
                    b = ((dy + 1) * 3 + k) * 128
                    wb[a:a + 128, 0:128] = w
                    wb[b:b + 128, 128:256] = w
            for wb in (wbe, wbo):
                wb[k * 128:(k + 1) * 128, 128:256] = zero
                wb[(9 + k) * 128:(10 + k) * 128, 0:128] = zero
        for dy in range(3):
            r = dy * 256
            wd[r:r + 128, 0:128] = dw_ref[dy, 0]
            wd[r + 128:r + 256, 0:128] = dw_ref[dy, 1]
            wd[r:r + 128, 128:256] = dw_ref[dy, 2]
            wd[r + 128:r + 256, 128:256] = zero

    pair = lax.broadcasted_iota(jnp.int32, (128, 128), 0)

    def from_before(p):
        return jnp.where(pair == 0, 0.0, pltpu.roll(p, 1, 0))

    def from_after(p):
        return jnp.where(pair == 127, 0.0, pltpu.roll(p, 127, 0))

    cb = jnp.concatenate([cb_ref[...], cb_ref[...]], axis=1)

    def dot(a, b):
        return jnp.dot(a, b, preferred_element_type=F32)

    def finish(y, t, own, even, odd):
        m = res[y][t].astype(F32) + cb + own
        for p, v in ((0, m[:, :128] + from_before(even)), (1, m[:, 128:] + from_after(odd))):
            if y == 16:
                v = jnp.where(tile == tiles - 1, 0.0, v)
            mix[y][t, :, p * 128:(p + 1) * 128] = v.astype(BF16)

    def conv_step(s):
        y = 2 * s
        n = 1 if s == 8 else 2
        for t in range(count):
            blocks = [
                jnp.concatenate([act[y + i + dy][3 * t + k] for dy in range(3) for k in range(3)], axis=1)
                for i in range(n)
            ]
            own = dot(jnp.concatenate(blocks, axis=0), wa[...])
            sides = []
            for p, wb in ((1, wbe), (0, wbo)):
                left = jnp.concatenate(
                    [act[y + q][3 * t + k, :, p * 128:(p + 1) * 128] for q in range(n + 2) for k in range(3)],
                    axis=1)
                sides.append(dot(left, wb[...] if n == 2 else wb[0:1152, 0:128]))
            for i in range(n):
                even, odd = (v[:, i * 128:(i + 1) * 128] for v in sides)
                finish(y + i, t, own[i * 128:(i + 1) * 128], even, odd)

    def out_row(r):
        left = jnp.concatenate(
            [jnp.concatenate([mix[2 * r + dy][t] for dy in range(3)], axis=1) for t in range(count)], axis=0)
        p = dot(left, wd[...])
        for t in range(count):
            q = p[t * 128:(t + 1) * 128]
            obuf[t, r] = (q[:, :128] + from_after(q[:, 128:]) + db_ref[...]).astype(BF16)

    act_step(0)
    build_weights()
    for s in range(9):
        conv_step(s)
        if s == 0:
            arrive(1)
        if s < 8:
            act_step(s + 1)
        if s >= 2:
            out_row(s - 2)
    out_row(7)
    copy = pltpu.make_async_copy(obuf, out_ref.at[pl.ds(target, 2)], osem)
    copy.start()
    copy.wait()


def two_frames(base, target, scalars, vectors, shared, big, groups, flops, unread):
    anywhere = pl.BlockSpec(memory_space=pl.ANY)
    vmem = pl.BlockSpec(memory_space=pltpu.VMEM)
    smem = pl.BlockSpec(memory_space=pltpu.SMEM)
    out = jax.ShapeDtypeStruct((4, 8, 128, 128), BF16)
    scratch = [
        pltpu.VMEM((4, 19, 256, 128), BF16),
        pltpu.VMEM((32, 256, 128), F32),
        pltpu.VMEM((2304, 256), BF16),
        pltpu.VMEM((1536, 256), BF16),
        pltpu.VMEM((1536, 256), BF16),
        pltpu.VMEM((768, 256), BF16),
        pltpu.VMEM((8, 128), F32),
        pltpu.VMEM((2, 8, 128, 128), BF16),
        pltpu.VMEM(shared[0].shape, F32),
        pltpu.VMEM(shared[1].shape, BF16),
        pltpu.VMEM(shared[2].shape, BF16),
        pltpu.SemaphoreType.DMA((3 + 4 * len(groups),)),
        pltpu.SemaphoreType.DMA,
    ]
    scratch += [pltpu.VMEM((6, 128, 256), BF16)] * 19
    scratch += [pltpu.VMEM((2, 128, 256), BF16)] * 34
    operands = [*scalars, *vectors, *shared, *big, *unread]
    specs = [smem] * len(scalars) + [vmem] * len(vectors) + [anywhere] * (len(shared) + len(big) + len(unread))
    return pl.pallas_call(
        functools.partial(block_kernel, base, target, (len(big) + len(unread), groups)),
        out_shape=out,
        in_specs=specs,
        out_specs=anywhere,
        scratch_shapes=scratch,
        input_output_aliases={len(operands) - 1: 0} if target == 0 else {},
        compiler_params=pltpu.CompilerParams(vmem_limit_bytes=VMEM_LIMIT),
        cost_estimate=pl.CostEstimate(flops=flops, bytes_accessed=6 * 2**20, transcendentals=10**7),
        name="two_frames",
    )(*operands)


def shards(frames, clip_frames, norm_gain, norm_bias, conv_weight, conv_bias, down_weight, down_bias):
    slabs, tiles = lax.axis_size("slab"), lax.axis_size("tile")
    both = ("slab", "tile")

    frames = pltpu.with_memory_space_constraint(frames, pltpu.HBM)

    def flat(s, t):
        return s * tiles + t

    sums, far, near, top, bottom, corner_top, corner_bottom = sums_and_rows(frames, slabs * tiles)
    sums = lax.all_to_all(sums, both, 0, 0)
    cells = [(s, t) for s in range(slabs - 1) for t in range(tiles - 1)]
    top = lax.ppermute(top, "tile", [(t, t + 1) for t in range(tiles - 1)])
    bottom = lax.ppermute(bottom, "tile", [(t + 1, t) for t in range(tiles - 1)])
    along = [(s, s + 1) for s in range(slabs - 1)]
    near = lax.ppermute(near, "slab", along)
    far = lax.ppermute(far, "slab", along)
    top_earlier = lax.ppermute(corner_top, both, [(flat(s, t), flat(s + 1, t + 1)) for s, t in cells])
    bottom_earlier = lax.ppermute(corner_bottom, both, [(flat(s, t + 1), flat(s + 1, t)) for s, t in cells])
    place = jnp.stack([lax.axis_index("slab"), lax.axis_index("tile"), jnp.int32(tiles)]).astype(jnp.int32)
    vectors = [v[None] for v in (norm_gain, norm_bias, conv_bias, down_bias)]
    scalars, shared = (place, clip_frames), (sums, conv_weight, down_weight)
    last = two_frames(
        0, 2, scalars, vectors, shared, (frames, top, bottom), [(0, 4, (0, 0), (1, 0), (2, 0))], FLOPS, (near,))
    groups = [
        (0, 1, (0, 0), (1, 0), (2, 0)),
        (1, 1, (3, 0), (1, 1), (2, 1)),
        (2, 2, (4, 0), (5, 0), (6, 0)),
    ]
    return two_frames(
        -2, 0, scalars, vectors, shared, (far, top_earlier, bottom_earlier, near, frames, top, bottom), groups, FLOPS,
        (last,))


def solution(mesh):
    return jax.shard_map(
        shards,
        mesh=mesh,
        in_specs=(P("slab", "tile", None, None), P(), P(), P(), P(), P(), P(), P()),
        out_specs=P("slab", "tile", None, None),
        check_vma=False,
    )
```

time: 78 us -> 63.1 us (0.81)
  Pallas kernels: 41.8 us -> 32.8 us
  local copies, waits for them, and re-layouts: 7.04 us -> 0.03 us
  starting transfers between devices: 26.3 us -> 28.3 us
    pallas_call x3, Pallas kernels: 41.8 us -> 32.8 us  [the longest x2 28.9 us: two_frames(): pl.pallas_call(functools.partial(block_kernel, base, target, (len(big) +...]
    slice x5 -> x0, local copies, waits for them, and re-layouts: 5.76 us -> none  [the longest x1 1.8 us: shards(): frames[2:4]]
    ppermute x5 -> x6, starting transfers between devices: 16.7 us -> 18.8 us  [the longest x1 5.27 us: shards(): lax.ppermute(corner_top, both, [(flat(s, t), flat(s + 1, t + 1)) for s, t...]
    unnamed x4 -> x14, local copies, waits for them, and re-layouts: 1.28 us -> 0.03 us
  transfers between devices with their start and end apart: 6 -> 7, of which waited for: 1 -> 1; matrix products, arithmetic and copies ran while one was open for 6% -> 0% of each run, Pallas kernels for 31% -> 23%
where the time goes in v1:
time: 63.1 us; the launch traced here: 62.6 us
  Pallas kernels  32.8 us (52%)
  starting transfers between devices  28.3 us (45%)
  waiting for transfers between devices  1.02 us (2%)
    pallas_call x2, Pallas kernels, two_frames(): pl.pallas_call(functools.partial(block_kernel, base, target, (len(big) +...  28.9 us
    all_to_all x1, starting transfers between devices, shards(): sums = lax.all_to_all(sums, both, 0, 0)  9.49 us
    ppermute x1, starting transfers between devices, shards(): lax.ppermute(corner_top, both, [(flat(s, t), flat(s + 1, t + 1)) for s, t...  5.27 us
    ppermute x1, starting transfers between devices, shards(): near = lax.ppermute(near, 'slab', along)  4.59 us
    ppermute x1, starting transfers between devices, shards(): top = lax.ppermute(top, 'tile', [(t, t + 1) for t in range(tiles - 1)])  4.18 us
    pallas_call x1, Pallas kernels, sums_and_rows(): pl.pallas_call(functools.partial(sums_kernel, pieces), in_specs=[anywhere...  3.94 us
    ppermute x1, starting transfers between devices, shards(): far = lax.ppermute(far, 'slab', along)  2.22 us
    ppermute x1, starting transfers between devices, shards(): lax.ppermute(bottom, 'tile', [(t + 1, t) for t in range(tiles - 1)])  1.29 us
  transfers between devices with their start and end apart: 7, of which 1 were waited for; matrix products, arithmetic and copies ran while one was open for 0% of the time, Pallas kernels for 23%

profile of v1, /device:TPU:1, one launch (start us, length us, event | category | flops | bytes accessed | tf_op | source)
XLA Modules:
  0.0 62.6 jit_solution(510447194810959969)
XLA Ops:
  0.0 0.0 copy-start.1
  0.0 0.0 copy-start
  0.0 0.0 copy-start.2
  0.0 0.0 copy-start.6
  0.0 0.0 copy-start.5
  0.0 0.0 copy-start.4
  0.0 0.0 copy-start.3
  0.0 3.9 %sums_and_rows.1 = (f32[128,2,128]{2,1,0:T(2,128)}, bf16[1,16,256,128]{3,2,1,0:T(8,128)(2,1)}, bf16[1,16,256,128]{3,2,1,0:T(8,128)(2,1)}, bf16[4,1,256,128]{3,2,...) custom-call(bf16[4,16,256,128]{3,2,1,0:T(8,128)(2,1)} %rest_4_.1), custom_call_target="tpu_custom_call" | custom-call | tf_op jit(solution)/shard_map/sums_and_rows/pallas_call | solution.py:80
  4.0 4.6 %collective-permute-start.3 = (bf16[1,16,256,128]{3,2,1,0:T(8,128)(2,1)}, bf16[1,16,256,128]{3,2,1,0:T(8,128)(2,1)S(1)}, u32[]{:S(2)}, u32[]{:S(2)}) collective-permute-start(bf16[1,16,256,128]{3,2,1,0:T(8,128)(2,1)} %get-tuple-element.16), channel_id=1, source_target_pairs={{0,4},{4,8},{8,12},{12,16},{16,20},{20,24},{24,28},{28,32},{32,36}... | collective-permute-start | bytes 3145736 | tf_op jit(solution)/shard_map/ppermute | solution.py:338
  8.6 1.3 %collective-permute-start.5 = (bf16[4,2,256,128]{3,2,1,0:T(8,128)(2,1)}, bf16[4,2,256,128]{3,2,1,0:T(8,128)(2,1)S(1)}, u32[]{:S(2)}, u32[]{:S(2)}) collective-permute-start(bf16[4,2,256,128]{3,2,1,0:T(8,128)(2,1)} %get-tuple-element.18), channel_id=1, source_target_pairs={{1,0},{2,1},{3,2},{5,4},{6,5},{7,6},{9,8},{10,9},{11,10},{13,12},{... | collective-permute-start | bytes 1572872 | tf_op jit(solution)/shard_map/ppermute | solution.py:336
  9.9 4.2 %collective-permute-start.4 = (bf16[4,1,256,128]{3,2,1,0:T(8,128)(2,1)}, bf16[4,1,256,128]{3,2,1,0:T(8,128)(2,1)S(1)}, u32[]{:S(2)}, u32[]{:S(2)}) collective-permute-start(bf16[4,1,256,128]{3,2,1,0:T(8,128)(2,1)} %get-tuple-element.17), channel_id=1, source_target_pairs={{0,1},{1,2},{2,3},{4,5},{5,6},{6,7},{8,9},{9,10},{10,11},{12,13},{... | collective-permute-start | bytes 786440 | tf_op jit(solution)/shard_map/ppermute | solution.py:335
  14.1 9.5 %all-to-all-start = ((f32[128,2,128]{2,1,0:T(2,128)}), f32[128,2,128]{2,1,0:T(2,128)S(1)}, u32[]{:S(2)}, u32[]{:S(2)}) async-start(f32[128,2,128]{2,1,0:T(2,128)} %get-tuple-element.12), calls=%async_computation | async-start | bytes 262144 | tf_op jit(solution)/shard_map/all_to_all | solution.py:333
  23.6 5.3 %collective-permute-start.1 = (bf16[2,1,256,128]{3,2,1,0:T(8,128)(2,1)}, bf16[2,1,256,128]{3,2,1,0:T(8,128)(2,1)}, u32[]{:S(2)}, u32[]{:S(2)}) collective-permute-start(bf16[2,1,256,128]{3,2,1,0:T(8,128)(2,1)} %get-tuple-element.14), channel_id=1, source_target_pairs={{0,5},{1,6},{2,7},{4,9},{5,10},{6,11},{8,13},{9,14},{10,15},{12,17... | collective-permute-start | bytes 393224 | tf_op jit(solution)/shard_map/ppermute | solution.py:340
  28.9 1.3 %collective-permute-start.2 = (bf16[2,2,256,128]{3,2,1,0:T(8,128)(2,1)}, bf16[2,2,256,128]{3,2,1,0:T(8,128)(2,1)}, u32[]{:S(2)}, u32[]{:S(2)}) collective-permute-start(bf16[2,2,256,128]{3,2,1,0:T(8,128)(2,1)} %get-tuple-element.15), channel_id=1, source_target_pairs={{1,4},{2,5},{3,6},{5,8},{6,9},{7,10},{9,12},{10,13},{11,14},{13,16... | collective-permute-start | bytes 786440 | tf_op jit(solution)/shard_map/ppermute | solution.py:341
  30.2 0.1 pad_add_fusion.pos_ref
  30.2 0.0 collective-permute-done.4.rest_1_.rest_5_
  30.2 2.2 %collective-permute-start = (bf16[1,16,256,128]{3,2,1,0:T(8,128)(2,1)}, bf16[1,16,256,128]{3,2,1,0:T(8,128)(2,1)}, u32[]{:S(2)}, u32[]{:S(2)}) collective-permute-start(bf16[1,16,256,128]{3,2,1,0:T(8,128)(2,1)} %get-tuple-element.13), channel_id=1, source_target_pairs={{0,4},{4,8},{8,12},{12,16},{16,20},{20,24},{24,28},{28,32},{32,36}... | collective-permute-start | bytes 3145736 | tf_op jit(solution)/shard_map/ppermute | solution.py:339
  32.5 1.0 %all-to-all-done.sums_hbm = f32[128,2,128]{2,1,0:T(2,128)S(1)} async-done(((f32[128,2,128]{2,1,0:T(2,128)}), f32[128,2,128]{2,1,0:T(2,128)S(1)}, u32[]{:S(2)}, u32[]{:S(2)}) %all-to-all-start) | async-done | bytes 131104 | tf_op jit(solution)/shard_map/all_to_all | solution.py:333
  33.5 0.0 collective-permute-done.5.rest_2_.rest_6_
  33.5 0.0 collective-permute-done.3.rest_3_
  33.5 0.0 copy-done.1
  33.5 0.0 copy-done
  33.5 0.0 copy-done.2
  33.5 0.0 copy-done.6
  33.5 0.0 copy-done.5
  33.5 0.0 copy-done.4
  33.5 0.0 copy-done.3
  33.5 14.3 %two_frames.2.rest_7_ = bf16[4,8,128,128]{3,2,1,0:T(8,128)(2,1)} custom-call(s32[3]{0:T(128)S(1)} %pad_add_fusion.pos_ref, s32[16]{0:T(128)S(1)} %copy-done.2, f32[1,128]{1,0:T(1,128)S(1)} %bitcast.6, f32[1,128]{1,0:T(1,128)S(1)} %bitcast.8, f32[1,128]{1,0:T(1,128)S(1)} %bitcast.10, f32[1,128]{1,0:T(1,128)S(1)} %bitcast.12, ...), custom_call_target="tpu_custom_call" | custom-call | flops 199999995904 | bytes 6291456 | tf_op jit(solution)/shard_map/two_frames/pallas_call | solution.py:310
  47.8 0.0 collective-permute-done.1.rest_1_
  47.8 0.0 collective-permute-done.2.rest_2_
  47.8 0.0 collective-permute-done.rest_0_
  47.9 14.6 %two_frames.3 = bf16[4,8,128,128]{3,2,1,0:T(8,128)(2,1)} custom-call(s32[3]{0:T(128)S(1)} %pad_add_fusion.pos_ref, s32[16]{0:T(128)S(1)} %copy-done.2, f32[1,128]{1,0:T(1,128)S(1)} %bitcast.7, f32[1,128]{1,0:T(1,128)S(1)} %bitcast.9, f32[1,128]{1,0:T(1,128)S(1)} %bitcast.11, f32[1,128]{1,0:T(1,128)S(1)} %bitcast.13, ...), custom_call_target="tpu_custom_call", output_to_operand_aliasing={{}: (16, {})} | custom-call | flops 199999995904 | bytes 6291456 | tf_op jit(solution)/shard_map/two_frames/pallas_call | solution.py:310
Async XLA Ops:
  0.0 33.5 %copy-start.1 = (bf16[3,3,128,128]{3,2,1,0:T(8,128)(2,1)S(1)}, bf16[3,3,128,128]{3,2,1,0:T(8,128)(2,1)}, u32[]{:S(2)}) copy-start(bf16[3,3,128,128]{3,2,1,0:T(8,128)(2,1)} %dw_hbm.3) | copy-start | bytes 884740
  0.0 33.5 %copy-start = (bf16[3,3,3,128,128]{4,3,2,1,0:T(8,128)(2,1)S(1)}, bf16[3,3,3,128,128]{4,3,2,1,0:T(8,128)(2,1)}, u32[]{:S(2)}) copy-start(bf16[3,3,3,128,128]{4,3,2,1,0:T(8,128)(2,1)} %w_hbm.3) | copy-start | bytes 2654212
  0.0 33.5 %copy-start.2 = (s32[16]{0:T(128)S(1)}, s32[16]{0:T(128)}, u32[]{:S(2)}) copy-start(s32[16]{0:T(128)} %clips_ref.3) | copy-start | bytes 196
  0.0 33.5 %copy-start.6 = (f32[128]{0:T(128)S(1)}, f32[128]{0:T(128)}, u32[]{:S(2)}) copy-start(f32[128]{0:T(128)} %param.15) | copy-start | bytes 1540
  0.0 33.5 %copy-start.5 = (f32[128]{0:T(128)S(1)}, f32[128]{0:T(128)}, u32[]{:S(2)}) copy-start(f32[128]{0:T(128)} %param.13) | copy-start | bytes 1540
  0.0 33.5 %copy-start.4 = (f32[128]{0:T(128)S(1)}, f32[128]{0:T(128)}, u32[]{:S(2)}) copy-start(f32[128]{0:T(128)} %param.11) | copy-start | bytes 1540
  0.0 33.5 %copy-start.3 = (f32[128]{0:T(128)S(1)}, f32[128]{0:T(128)}, u32[]{:S(2)}) copy-start(f32[128]{0:T(128)} %param.10) | copy-start | bytes 1540
  4.0 29.5 %collective-permute-start.3 = (bf16[1,16,256,128]{3,2,1,0:T(8,128)(2,1)}, bf16[1,16,256,128]{3,2,1,0:T(8,128)(2,1)S(1)}, u32[]{:S(2)}, u32[]{:S(2)}) collective-permute-start(bf16[1,16,256,128]{3,2,1,0:T(8,128)(2,1)} %get-tuple-element.16), channel_id=1, source_target_pairs={{0,4},{4,8},{8,12},{12,16},{16,20},{20,24},{24,28},{28,32},{32,36}... | collective-permute-start | bytes 3145736 | tf_op jit(solution)/shard_map/ppermute | solution.py:338
  8.6 24.9 %collective-permute-start.5 = (bf16[4,2,256,128]{3,2,1,0:T(8,128)(2,1)}, bf16[4,2,256,128]{3,2,1,0:T(8,128)(2,1)S(1)}, u32[]{:S(2)}, u32[]{:S(2)}) collective-permute-start(bf16[4,2,256,128]{3,2,1,0:T(8,128)(2,1)} %get-tuple-element.18), channel_id=1, source_target_pairs={{1,0},{2,1},{3,2},{5,4},{6,5},{7,6},{9,8},{10,9},{11,10},{13,12},{... | collective-permute-start | bytes 1572872 | tf_op jit(solution)/shard_map/ppermute | solution.py:336
  9.9 20.3 %collective-permute-start.4 = (bf16[4,1,256,128]{3,2,1,0:T(8,128)(2,1)}, bf16[4,1,256,128]{3,2,1,0:T(8,128)(2,1)S(1)}, u32[]{:S(2)}, u32[]{:S(2)}) collective-permute-start(bf16[4,1,256,128]{3,2,1,0:T(8,128)(2,1)} %get-tuple-element.17), channel_id=1, source_target_pairs={{0,1},{1,2},{2,3},{4,5},{5,6},{6,7},{8,9},{9,10},{10,11},{12,13},{... | collective-permute-start | bytes 786440 | tf_op jit(solution)/shard_map/ppermute | solution.py:335
  14.1 19.4 %all-to-all-start = ((f32[128,2,128]{2,1,0:T(2,128)}), f32[128,2,128]{2,1,0:T(2,128)S(1)}, u32[]{:S(2)}, u32[]{:S(2)}) async-start(f32[128,2,128]{2,1,0:T(2,128)} %get-tuple-element.12), calls=%async_computation | async-start | bytes 262144 | tf_op jit(solution)/shard_map/all_to_all | solution.py:333
  23.6 24.2 %collective-permute-start.1 = (bf16[2,1,256,128]{3,2,1,0:T(8,128)(2,1)}, bf16[2,1,256,128]{3,2,1,0:T(8,128)(2,1)}, u32[]{:S(2)}, u32[]{:S(2)}) collective-permute-start(bf16[2,1,256,128]{3,2,1,0:T(8,128)(2,1)} %get-tuple-element.14), channel_id=1, source_target_pairs={{0,5},{1,6},{2,7},{4,9},{5,10},{6,11},{8,13},{9,14},{10,15},{12,17... | collective-permute-start | bytes 393224 | tf_op jit(solution)/shard_map/ppermute | solution.py:340
  28.9 19.0 %collective-permute-start.2 = (bf16[2,2,256,128]{3,2,1,0:T(8,128)(2,1)}, bf16[2,2,256,128]{3,2,1,0:T(8,128)(2,1)}, u32[]{:S(2)}, u32[]{:S(2)}) collective-permute-start(bf16[2,2,256,128]{3,2,1,0:T(8,128)(2,1)} %get-tuple-element.15), channel_id=1, source_target_pairs={{1,4},{2,5},{3,6},{5,8},{6,9},{7,10},{9,12},{10,13},{11,14},{13,16... | collective-permute-start | bytes 786440 | tf_op jit(solution)/shard_map/ppermute | solution.py:341
  30.2 17.6 %collective-permute-start = (bf16[1,16,256,128]{3,2,1,0:T(8,128)(2,1)}, bf16[1,16,256,128]{3,2,1,0:T(8,128)(2,1)}, u32[]{:S(2)}, u32[]{:S(2)}) collective-permute-start(bf16[1,16,256,128]{3,2,1,0:T(8,128)(2,1)} %get-tuple-element.13), channel_id=1, source_target_pairs={{0,4},{4,8},{8,12},{12,16},{16,20},{20,24},{24,28},{28,32},{32,36}... | collective-permute-start | bytes 3145736 | tf_op jit(solution)/shard_map/ppermute | solution.py:339

commit v2 on v1

--- a/solution.py
+++ b/solution.py
@@ -25,7 +25,7 @@
     return out[:n] + out[n:2 * n] + out[2 * n:]
 
 
-def sums_kernel(pieces, x_ref, out_ref, far_ref, near_ref, top_ref, bottom_ref, corner_top_ref, corner_bottom_ref, xin, load, store):
+def sums_kernel(pieces, x_ref, out_ref, far_ref, near_ref, top_ref, bottom_ref, xin, load, store):
     count, rows, cols, chans = x_ref.shape
     part = rows // pieces
     order = [2, 3, 0, 1]
@@ -52,9 +52,7 @@
                 send(xin.at[f, pl.ds(0, 2)], bottom_ref.at[f])
                 send(xin.at[f, pl.ds(rows - 1, 1)], top_ref.at[f])
                 if f >= 2:
-                    send(xin.at[f], (far_ref, near_ref)[f - 2].at[0])
-                    send(xin.at[f, pl.ds(0, 2)], corner_bottom_ref.at[f - 2])
-                    send(xin.at[f, pl.ds(rows - 1, 1)], corner_top_ref.at[f - 2])
+                    send(xin.at[f], (far_ref.at[0, pl.ds(0, rows)], near_ref.at[0])[f - 2])
 
             def row(i, both, f=f, p=p):
                 x = xin[f, p * part + i].astype(F32).reshape(cols // 32, 32, chans)
@@ -76,17 +74,17 @@
     count, rows, cols, chans = frames.shape
     pieces = 4
     anywhere = pl.BlockSpec(memory_space=pl.ANY)
-    shapes = [(1, rows), (1, rows), (count, 1), (count, 2), (2, 1), (2, 2)]
+    shapes = [(1, rows + 6), (1, rows), (count, 1), (count, 2)]
     return pl.pallas_call(
         functools.partial(sums_kernel, pieces),
         in_specs=[anywhere],
-        out_specs=[pl.BlockSpec(memory_space=pltpu.VMEM)] + [anywhere] * 6,
+        out_specs=[pl.BlockSpec(memory_space=pltpu.VMEM)] + [anywhere] * 4,
         out_shape=[jax.ShapeDtypeStruct((devices, 2, chans), F32)]
         + [jax.ShapeDtypeStruct(s + (cols, chans), BF16) for s in shapes],
         scratch_shapes=[
             pltpu.VMEM((count, rows, cols, chans), BF16),
             pltpu.SemaphoreType.DMA((count * pieces,)),
-            pltpu.SemaphoreType.DMA((14,)),
+            pltpu.SemaphoreType.DMA((10,)),
         ],
         compiler_params=pltpu.CompilerParams(vmem_limit_bytes=60 * 1024 * 1024),
         name="sums_and_rows",
@@ -94,14 +92,14 @@
 
 
 def block_kernel(
-    base, target, groups, pos_ref, clips_ref, gain_ref, bias_ref, cb_ref, db_ref, sums_hbm, w_hbm, dw_hbm, *rest,
+    base, target, groups, scalars, gain_ref, bias_ref, cb_ref, db_ref, sums_ref, w_ref, dw_ref, *rest,
 ):
     inputs, rest = rest[:groups[0]], rest[groups[0]:]
-    out_ref, xin, xs, wa, wbe, wbo, wd, vsum, obuf, sums_ref, w_ref, dw_ref, sems, osem = rest[:14]
-    rows = rest[14:]
+    out_ref, xin, xs, wa, wbe, wbo, wd, vsum, obuf, sems, osems = rest[:11]
+    rows = rest[11:]
     act, res, mix = rows[:19], rows[19:36], rows[36:]
     count, slots = 2, 4
-    slab, tile, tiles = pos_ref[0], pos_ref[1], pos_ref[2]
+    slab, tile, tiles = scalars[0], scalars[1], scalars[2]
 
     copies = {}
     used = [0]
@@ -118,15 +116,12 @@
 
     def fetch(step, which, first_row, number, at):
         for slot, n, *places in groups[1]:
-            ref, index = places[which]
-            src = inputs[ref].at[pl.ds(index, n), pl.ds(first_row, number)]
+            ref, index, row = places[which]
+            src = inputs[ref].at[pl.ds(index, n), pl.ds(row + first_row, number)]
             start(step, src, xin.at[pl.ds(slot, n), pl.ds(at, number)])
 
-    start(0, sums_hbm, sums_ref)
     fetch(0, 1, 0, 1, 0)
     fetch(0, 0, 0, 3, 1)
-    start(0, w_hbm, w_ref)
-    start(0, dw_hbm, dw_ref)
     fetch(1, 0, 3, 13, 4)
     fetch(1, 2, 0, 2, 17)
 
@@ -134,8 +129,8 @@
     starts = [jnp.int32(0)] * slots
     ends = [jnp.int32(1)] * slots
     begin = jnp.int32(0)
-    for c in range(clips_ref.shape[0]):
-        end = begin + clips_ref[c]
+    for c in range(3, scalars.shape[0]):
+        end = begin + scalars[c]
         for f in range(slots):
             inside = (begin <= first + f) & (first + f < end)
             starts[f] = jnp.where(inside, begin, starts[f])
@@ -144,7 +139,6 @@
     opens = [starts[f] == first + f for f in range(slots)]
     second = [starts[f] == first + f - 1 for f in range(slots)]
 
-    arrive(0)
     slabs = sums_ref.shape[0] // 4
     sums = jnp.sum(sums_ref[...].reshape(slabs, 4, 2, 128), axis=1)
     frame_of = 4 * lax.broadcasted_iota(jnp.int32, (slabs, 2, 128), 0) + (
@@ -267,8 +261,17 @@
             q = p[t * 128:(t + 1) * 128]
             obuf[t, r] = (q[:, :128] + from_after(q[:, 128:]) + db_ref[...]).astype(BF16)
 
+    leaving = []
+
+    def leave(first_row, number):
+        cut = pl.ds(first_row, number)
+        copy = pltpu.make_async_copy(obuf.at[:, cut], out_ref.at[pl.ds(target, 2), cut], osems.at[len(leaving)])
+        copy.start()
+        leaving.append(copy)
+
+    build_weights()
+    arrive(0)
     act_step(0)
-    build_weights()
     for s in range(9):
         conv_step(s)
         if s == 0:
@@ -277,15 +280,15 @@
             act_step(s + 1)
         if s >= 2:
             out_row(s - 2)
+    leave(0, 7)
     out_row(7)
-    copy = pltpu.make_async_copy(obuf, out_ref.at[pl.ds(target, 2)], osem)
-    copy.start()
-    copy.wait()
+    leave(7, 1)
+    for copy in leaving:
+        copy.wait()
 
 
 def two_frames(base, target, scalars, vectors, shared, big, groups, flops, unread):
     anywhere = pl.BlockSpec(memory_space=pl.ANY)
-    vmem = pl.BlockSpec(memory_space=pltpu.VMEM)
     smem = pl.BlockSpec(memory_space=pltpu.SMEM)
     out = jax.ShapeDtypeStruct((4, 8, 128, 128), BF16)
     scratch = [
@@ -297,16 +300,14 @@
         pltpu.VMEM((768, 256), BF16),
         pltpu.VMEM((8, 128), F32),
         pltpu.VMEM((2, 8, 128, 128), BF16),
-        pltpu.VMEM(shared[0].shape, F32),
-        pltpu.VMEM(shared[1].shape, BF16),
-        pltpu.VMEM(shared[2].shape, BF16),
-        pltpu.SemaphoreType.DMA((3 + 4 * len(groups),)),
-        pltpu.SemaphoreType.DMA,
+        pltpu.SemaphoreType.DMA((4 * len(groups),)),
+        pltpu.SemaphoreType.DMA((2,)),
     ]
     scratch += [pltpu.VMEM((6, 128, 256), BF16)] * 19
     scratch += [pltpu.VMEM((2, 128, 256), BF16)] * 34
-    operands = [*scalars, *vectors, *shared, *big, *unread]
-    specs = [smem] * len(scalars) + [vmem] * len(vectors) + [anywhere] * (len(shared) + len(big) + len(unread))
+    operands = [scalars, *vectors, *shared, *big, *unread]
+    near_by = len(vectors) + len(shared)
+    specs = [smem] + [pl.BlockSpec(memory_space=pltpu.VMEM)] * near_by + [anywhere] * (len(big) + len(unread))
     return pl.pallas_call(
         functools.partial(block_kernel, base, target, (len(big) + len(unread), groups)),
         out_shape=out,
@@ -325,33 +326,26 @@
     both = ("slab", "tile")
 
     frames = pltpu.with_memory_space_constraint(frames, pltpu.HBM)
-
-    def flat(s, t):
-        return s * tiles + t
-
-    sums, far, near, top, bottom, corner_top, corner_bottom = sums_and_rows(frames, slabs * tiles)
+    sums, far, near, top, bottom = sums_and_rows(frames, slabs * tiles)
     sums = lax.all_to_all(sums, both, 0, 0)
-    cells = [(s, t) for s in range(slabs - 1) for t in range(tiles - 1)]
     top = lax.ppermute(top, "tile", [(t, t + 1) for t in range(tiles - 1)])
     bottom = lax.ppermute(bottom, "tile", [(t + 1, t) for t in range(tiles - 1)])
     along = [(s, s + 1) for s in range(slabs - 1)]
     near = lax.ppermute(near, "slab", along)
+    corners = [top[2:4].reshape(1, 2, *top.shape[2:]), bottom[2:4].reshape(1, 4, *bottom.shape[2:])]
+    far = lax.dynamic_update_slice(far, jnp.concatenate(corners, axis=1), (0, 16, 0, 0))
     far = lax.ppermute(far, "slab", along)
-    top_earlier = lax.ppermute(corner_top, both, [(flat(s, t), flat(s + 1, t + 1)) for s, t in cells])
-    bottom_earlier = lax.ppermute(corner_bottom, both, [(flat(s, t + 1), flat(s + 1, t)) for s, t in cells])
     place = jnp.stack([lax.axis_index("slab"), lax.axis_index("tile"), jnp.int32(tiles)]).astype(jnp.int32)
+    scalars, shared = jnp.concatenate([place, clip_frames]), (sums, conv_weight, down_weight)
     vectors = [v[None] for v in (norm_gain, norm_bias, conv_bias, down_bias)]
-    scalars, shared = (place, clip_frames), (sums, conv_weight, down_weight)
     last = two_frames(
-        0, 2, scalars, vectors, shared, (frames, top, bottom), [(0, 4, (0, 0), (1, 0), (2, 0))], FLOPS, (near,))
+        0, 2, scalars, vectors, shared, (frames, top, bottom), [(0, 4, (0, 0, 0), (1, 0, 0), (2, 0, 0))], FLOPS, (near,))
     groups = [
-        (0, 1, (0, 0), (1, 0), (2, 0)),
-        (1, 1, (3, 0), (1, 1), (2, 1)),
-        (2, 2, (4, 0), (5, 0), (6, 0)),
+        (0, 1, (0, 0, 0), (0, 0, 16), (0, 0, 18)),
+        (1, 1, (1, 0, 0), (0, 0, 17), (0, 0, 20)),
+        (2, 2, (2, 0, 0), (3, 0, 0), (4, 0, 0)),
     ]
-    return two_frames(
-        -2, 0, scalars, vectors, shared, (far, top_earlier, bottom_earlier, near, frames, top, bottom), groups, FLOPS,
-        (last,))
+    return two_frames(-2, 0, scalars, vectors, shared, (far, near, frames, top, bottom), groups, FLOPS, (last,))
 
 
 def solution(mesh):

time: 63.1 us -> 61.3 us (0.971)
  starting transfers between devices: 28.3 us -> 23.2 us
  waiting for transfers between devices: 1.02 us -> 5.4 us
  Pallas kernels: 32.8 us -> 31.2 us
  other arithmetic: 0.08 us -> 0.86 us
    ppermute x2 -> x0, starting transfers between devices: 6.55 us -> none  [the longest x1 5.27 us: shards(): lax.ppermute(corner_top, both, [(flat(s, t), flat(s + 1, t + 1)) for s, t...]
    all_to_all x1, waiting for transfers between devices: 1.01 us -> 5.39 us  [shards(): sums = lax.all_to_all(sums, both, 0, 0)]
    pallas_call x2, Pallas kernels: 28.9 us -> 27.3 us  [two_frames(): pl.pallas_call(functools.partial(block_kernel, base, target, (len(big) +...]
    ppermute x1, starting transfers between devices: 2.22 us -> 3.53 us  [shards(): far = lax.ppermute(far, 'slab', along)]
    dynamic_update_slice x0 -> x1, other arithmetic: none -> 0.79 us  [shards(): lax.dynamic_update_slice(far, jnp.concatenate(corners, axis=1), (0, 16, 0...]
  transfers between devices with their start and end apart: 7 -> 5, of which waited for: 1 -> 1; matrix products, arithmetic and copies ran while one was open for 0% -> 1% of each run, Pallas kernels for 23% -> 22%
where the time goes in v2:
time: 61.3 us; the launch traced here: 61.1 us
  Pallas kernels  31.2 us (51%)
  starting transfers between devices  23.2 us (38%)
  waiting for transfers between devices  5.4 us (9%)
  other arithmetic  0.86 us (1%)
    pallas_call x2, Pallas kernels, two_frames(): pl.pallas_call(functools.partial(block_kernel, base, target, (len(big) +...  27.3 us
    all_to_all x1, starting transfers between devices, shards(): sums = lax.all_to_all(sums, both, 0, 0)  9.49 us
    all_to_all x1, waiting for transfers between devices, shards(): sums = lax.all_to_all(sums, both, 0, 0)  5.39 us
    ppermute x1, starting transfers between devices, shards(): near = lax.ppermute(near, 'slab', along)  4.73 us
    ppermute x1, starting transfers between devices, shards(): top = lax.ppermute(top, 'tile', [(t, t + 1) for t in range(tiles - 1)])  4.18 us
    pallas_call x1, Pallas kernels, sums_and_rows(): pl.pallas_call(functools.partial(sums_kernel, pieces), in_specs=[anywhere...  3.82 us
    ppermute x1, starting transfers between devices, shards(): far = lax.ppermute(far, 'slab', along)  3.53 us
    ppermute x1, starting transfers between devices, shards(): lax.ppermute(bottom, 'tile', [(t + 1, t) for t in range(tiles - 1)])  1.29 us
  transfers between devices with their start and end apart: 5, of which 1 were waited for; matrix products, arithmetic and copies ran while one was open for 1% of the time, Pallas kernels for 22%

profile of v2, /device:TPU:1, one launch (start us, length us, event | category | flops | bytes accessed | tf_op | source)
XLA Modules:
  0.0 61.1 jit_solution(15701676026735954778)
XLA Ops:
  0.0 0.0 copy-start.6
  0.0 3.8 %sums_and_rows.1 = (f32[128,2,128]{2,1,0:T(2,128)}, bf16[1,22,256,128]{3,2,1,0:T(8,128)(2,1)}, bf16[1,16,256,128]{3,2,1,0:T(8,128)(2,1)}, bf16[4,1,256,128]{3,2,1,0:T(8,128)(2,1)}, bf16[4,2,256,128]{3,2,1,0:T(8,128)(2,1)}) custom-call(bf16[4,16,256,128]{3,2,1,0:T(8,128)(2,1)} %rest_2_.1), custom_call_target="tpu_custom_call" | custom-call | tf_op jit(solution)/shard_map/sums_and_rows/pallas_call | solution.py:78
  3.8 0.0 copy-start
  3.8 0.0 copy-start.1
  3.9 0.0 copy-start.2
  3.9 0.0 copy-start.3
  3.9 0.0 copy-start.4
  3.9 0.0 copy-start.5
  3.9 4.7 %collective-permute-start.3 = (bf16[1,16,256,128]{3,2,1,0:T(8,128)(2,1)}, bf16[1,16,256,128]{3,2,1,0:T(8,128)(2,1)S(1)}, u32[]{:S(2)}, u32[]{:S(2)}) collective-permute-start(bf16[1,16,256,128]{3,2,1,0:T(8,128)(2,1)} %get-tuple-element.14), channel_id=1, source_target_pairs={{0,4},{4,8},{8,12},{12,16},{16,20},{20,24},{24,28},{28,32},{32,36}... | collective-permute-start | bytes 3145736 | tf_op jit(solution)/shard_map/ppermute | solution.py:334
  8.6 1.3 %collective-permute-start.1 = (bf16[4,2,256,128]{3,2,1,0:T(8,128)(2,1)}, bf16[4,2,256,128]{3,2,1,0:T(8,128)(2,1)S(1)}, u32[]{:S(2)}, u32[]{:S(2)}) collective-permute-start(bf16[4,2,256,128]{3,2,1,0:T(8,128)(2,1)} %get-tuple-element.13), channel_id=1, source_target_pairs={{1,0},{2,1},{3,2},{5,4},{6,5},{7,6},{9,8},{10,9},{11,10},{13,12},{... | collective-permute-start | bytes 1572872 | tf_op jit(solution)/shard_map/ppermute | solution.py:332
  9.9 4.2 %collective-permute-start = (bf16[4,1,256,128]{3,2,1,0:T(8,128)(2,1)}, bf16[4,1,256,128]{3,2,1,0:T(8,128)(2,1)S(1)}, u32[]{:S(2)}, u32[]{:S(2)}) collective-permute-start(bf16[4,1,256,128]{3,2,1,0:T(8,128)(2,1)} %get-tuple-element.12), channel_id=1, source_target_pairs={{0,1},{1,2},{2,3},{4,5},{5,6},{6,7},{8,9},{9,10},{10,11},{12,13},{... | collective-permute-start | bytes 786440 | tf_op jit(solution)/shard_map/ppermute | solution.py:331
  14.1 9.5 %all-to-all-start = ((f32[128,2,128]{2,1,0:T(2,128)}), f32[128,2,128]{2,1,0:T(2,128)S(1)}, u32[]{:S(2)}, u32[]{:S(2)}) async-start(f32[128,2,128]{2,1,0:T(2,128)} %get-tuple-element.10), calls=%async_computation | async-start | bytes 262144 | tf_op jit(solution)/shard_map/all_to_all | solution.py:330
  23.6 0.0 copy-done.6
  23.6 0.1 pad_add_fusion.scalars
  23.7 0.0 collective-permute-done.rest_1_.rest_3_
  23.7 0.0 collective-permute-done.1.rest_2_.rest_4_
  23.8 0.8 %maximum_dynamic-update-slice_fusion = bf16[1,22,256,128]{3,2,1,0:T(8,128)(2,1)} fusion(bf16[1,22,256,128]{3,2,1,0:T(8,128)(2,1)} %get-tuple-element.11, bf16[1,4,256,128]{3,2,1,0:T(8,128)(2,1)S(1)} %bitcast.17, bf16[1,2,256,128]{3,2,1,0:T(8,128)(2,1)S(1)} %slice_bitcast_fusion), kind=kLoop, calls=%fused_computation | loop fusion | flops 786432 | bytes 786432 | tf_op jit(solution)/shard_map/dynamic_update_slice | solution.py:336
  24.6 3.5 %collective-permute-start.2 = (bf16[1,22,256,128]{3,2,1,0:T(8,128)(2,1)}, bf16[1,22,256,128]{3,2,1,0:T(8,128)(2,1)}, u32[]{:S(2)}, u32[]{:S(2)}) collective-permute-start(bf16[1,22,256,128]{3,2,1,0:T(8,128)(2,1)} %maximum_dynamic-update-slice_fusion), channel_id=1, source_target_pairs={{0,4},{4,8},{8,12},{12,16},{16,20},{20,24},{24,28},{28,32},{32,36}... | collective-permute-start | bytes 4325384 | tf_op jit(solution)/shard_map/ppermute | solution.py:337
  28.1 5.4 %all-to-all-done.sums_ref = f32[128,2,128]{2,1,0:T(2,128)S(1)} async-done(((f32[128,2,128]{2,1,0:T(2,128)}), f32[128,2,128]{2,1,0:T(2,128)S(1)}, u32[]{:S(2)}, u32[]{:S(2)}) %all-to-all-start) | async-done | bytes 131104 | tf_op jit(solution)/shard_map/all_to_all | solution.py:330
  33.5 0.0 collective-permute-done.3.rest_3_.rest_1_
  33.5 0.0 copy-done
  33.5 0.0 copy-done.1
  33.5 0.0 copy-done.2
  33.5 0.0 copy-done.3
  33.5 0.0 copy-done.4
  33.5 0.0 copy-done.5
  33.6 13.5 %two_frames.2.rest_5_ = bf16[4,8,128,128]{3,2,1,0:T(8,128)(2,1)} custom-call(s32[19]{0:T(128)S(1)} %pad_add_fusion.scalars, f32[1,128]{1,0:T(1,128)S(1)} %bitcast.9, f32[1,128]{1,0:T(1,128)S(1)} %bitcast.11, f32[1,128]{1,0:T(1,128)S(1)} %bitcast.13, f32[1,128]{1,0:T(1,128)S(1)} %bitcast.15, f32[128,2,128]{2,1,0:T(2,128)S(1)} %all-to-all-done.sums_ref, ...), custom_call_target="tpu_custom_call" | custom-call | flops 199999995904 | bytes 6291456 | tf_op jit(solution)/shard_map/two_frames/pallas_call | solution.py:311
  47.1 0.0 collective-permute-done.2.rest_0_
  47.1 13.8 %two_frames.3 = bf16[4,8,128,128]{3,2,1,0:T(8,128)(2,1)} custom-call(s32[19]{0:T(128)S(1)} %pad_add_fusion.scalars, f32[1,128]{1,0:T(1,128)S(1)} %bitcast.10, f32[1,128]{1,0:T(1,128)S(1)} %bitcast.12, f32[1,128]{1,0:T(1,128)S(1)} %bitcast.14, f32[1,128]{1,0:T(1,128)S(1)} %bitcast.16, ...), custom_call_target="tpu_custom_call", output_to_operand_aliasing={{}: (13, {})} | custom-call | flops 199999995904 | bytes 6291456 | tf_op jit(solution)/shard_map/two_frames/pallas_call | solution.py:311
  (2 shorter events, 0.0 us)
Async XLA Ops:
  0.0 23.6 %copy-start.6 = (s32[16]{0:T(128)S(1)}, s32[16]{0:T(128)}, u32[]{:S(2)}) copy-start(s32[16]{0:T(128)} %param.9) | copy-start | bytes 196
  3.8 29.7 %copy-start = (bf16[3,3,3,128,128]{4,3,2,1,0:T(8,128)(2,1)S(1)}, bf16[3,3,3,128,128]{4,3,2,1,0:T(8,128)(2,1)}, u32[]{:S(2)}) copy-start(bf16[3,3,3,128,128]{4,3,2,1,0:T(8,128)(2,1)} %w_ref.3) | copy-start | bytes 2654212
  3.8 29.7 %copy-start.1 = (bf16[3,3,128,128]{3,2,1,0:T(8,128)(2,1)S(1)}, bf16[3,3,128,128]{3,2,1,0:T(8,128)(2,1)}, u32[]{:S(2)}) copy-start(bf16[3,3,128,128]{3,2,1,0:T(8,128)(2,1)} %dw_ref.3) | copy-start | bytes 884740
  3.9 29.7 %copy-start.2 = (f32[128]{0:T(128)S(1)}, f32[128]{0:T(128)}, u32[]{:S(2)}) copy-start(f32[128]{0:T(128)} %param.10) | copy-start | bytes 1540
  3.9 29.7 %copy-start.3 = (f32[128]{0:T(128)S(1)}, f32[128]{0:T(128)}, u32[]{:S(2)}) copy-start(f32[128]{0:T(128)} %param.11) | copy-start | bytes 1540
  3.9 29.7 %copy-start.4 = (f32[128]{0:T(128)S(1)}, f32[128]{0:T(128)}, u32[]{:S(2)}) copy-start(f32[128]{0:T(128)} %param.13) | copy-start | bytes 1540
  3.9 29.7 %copy-start.5 = (f32[128]{0:T(128)S(1)}, f32[128]{0:T(128)}, u32[]{:S(2)}) copy-start(f32[128]{0:T(128)} %param.15) | copy-start | bytes 1540
  3.9 29.6 %collective-permute-start.3 = (bf16[1,16,256,128]{3,2,1,0:T(8,128)(2,1)}, bf16[1,16,256,128]{3,2,1,0:T(8,128)(2,1)S(1)}, u32[]{:S(2)}, u32[]{:S(2)}) collective-permute-start(bf16[1,16,256,128]{3,2,1,0:T(8,128)(2,1)} %get-tuple-element.14), channel_id=1, source_target_pairs={{0,4},{4,8},{8,12},{12,16},{16,20},{20,24},{24,28},{28,32},{32,36}... | collective-permute-start | bytes 3145736 | tf_op jit(solution)/shard_map/ppermute | solution.py:334
  8.6 15.1 %collective-permute-start.1 = (bf16[4,2,256,128]{3,2,1,0:T(8,128)(2,1)}, bf16[4,2,256,128]{3,2,1,0:T(8,128)(2,1)S(1)}, u32[]{:S(2)}, u32[]{:S(2)}) collective-permute-start(bf16[4,2,256,128]{3,2,1,0:T(8,128)(2,1)} %get-tuple-element.13), channel_id=1, source_target_pairs={{1,0},{2,1},{3,2},{5,4},{6,5},{7,6},{9,8},{10,9},{11,10},{13,12},{... | collective-permute-start | bytes 1572872 | tf_op jit(solution)/shard_map/ppermute | solution.py:332
  9.9 13.8 %collective-permute-start = (bf16[4,1,256,128]{3,2,1,0:T(8,128)(2,1)}, bf16[4,1,256,128]{3,2,1,0:T(8,128)(2,1)S(1)}, u32[]{:S(2)}, u32[]{:S(2)}) collective-permute-start(bf16[4,1,256,128]{3,2,1,0:T(8,128)(2,1)} %get-tuple-element.12), channel_id=1, source_target_pairs={{0,1},{1,2},{2,3},{4,5},{5,6},{6,7},{8,9},{9,10},{10,11},{12,13},{... | collective-permute-start | bytes 786440 | tf_op jit(solution)/shard_map/ppermute | solution.py:331
  14.1 19.4 %all-to-all-start = ((f32[128,2,128]{2,1,0:T(2,128)}), f32[128,2,128]{2,1,0:T(2,128)S(1)}, u32[]{:S(2)}, u32[]{:S(2)}) async-start(f32[128,2,128]{2,1,0:T(2,128)} %get-tuple-element.10), calls=%async_computation | async-start | bytes 262144 | tf_op jit(solution)/shard_map/all_to_all | solution.py:330
  24.6 22.5 %collective-permute-start.2 = (bf16[1,22,256,128]{3,2,1,0:T(8,128)(2,1)}, bf16[1,22,256,128]{3,2,1,0:T(8,128)(2,1)}, u32[]{:S(2)}, u32[]{:S(2)}) collective-permute-start(bf16[1,22,256,128]{3,2,1,0:T(8,128)(2,1)} %maximum_dynamic-update-slice_fusion), channel_id=1, source_target_pairs={{0,4},{4,8},{8,12},{12,16},{16,20},{20,24},{24,28},{28,32},{32,36}... | collective-permute-start | bytes 4325384 | tf_op jit(solution)/shard_map/ppermute | solution.py:337

commit v3 on v2

--- a/solution.py
+++ b/solution.py
@@ -278,11 +278,11 @@
             arrive(1)
         if s < 8:
             act_step(s + 1)
-        if s >= 2:
-            out_row(s - 2)
-    leave(0, 7)
-    out_row(7)
-    leave(7, 1)
+    for r in range(8):
+        out_row(r)
+        if r == 5:
+            leave(0, 6)
+    leave(6, 2)
     for copy in leaving:
         copy.wait()
 

time: 61.3 us -> 60.7 us (level)
  no operation moved by 1% of the time
where the time goes in v3:
time: 60.7 us; the launch traced here: 60.5 us
  Pallas kernels  30.6 us (50%)
  starting transfers between devices  23.2 us (38%)
  waiting for transfers between devices  5.4 us (9%)
  other arithmetic  0.86 us (1%)
    pallas_call x2, Pallas kernels, two_frames(): pl.pallas_call(functools.partial(block_kernel, base, target, (len(big) +...  26.7 us
    all_to_all x1, starting transfers between devices, shards(): sums = lax.all_to_all(sums, both, 0, 0)  9.49 us
    all_to_all x1, waiting for transfers between devices, shards(): sums = lax.all_to_all(sums, both, 0, 0)  5.39 us
    ppermute x1, starting transfers between devices, shards(): near = lax.ppermute(near, 'slab', along)  4.73 us
    ppermute x1, starting transfers between devices, shards(): top = lax.ppermute(top, 'tile', [(t, t + 1) for t in range(tiles - 1)])  4.18 us
    pallas_call x1, Pallas kernels, sums_and_rows(): pl.pallas_call(functools.partial(sums_kernel, pieces), in_specs=[anywhere...  3.82 us
    ppermute x1, starting transfers between devices, shards(): far = lax.ppermute(far, 'slab', along)  3.53 us
    ppermute x1, starting transfers between devices, shards(): lax.ppermute(bottom, 'tile', [(t + 1, t) for t in range(tiles - 1)])  1.29 us
  transfers between devices with their start and end apart: 5, of which 1 were waited for; matrix products, arithmetic and copies ran while one was open for 1% of the time, Pallas kernels for 22%

profile of v3, /device:TPU:1, one launch (start us, length us, event | category | flops | bytes accessed | tf_op | source)
XLA Modules:
  0.0 60.5 jit_solution(1079480034119723468)
XLA Ops:
  0.0 0.0 copy-start.6
  0.0 3.8 %sums_and_rows.1 = (f32[128,2,128]{2,1,0:T(2,128)}, bf16[1,22,256,128]{3,2,1,0:T(8,128)(2,1)}, bf16[1,16,256,128]{3,2,1,0:T(8,128)(2,1)}, bf16[4,1,256,128]{3,2,1,0:T(8,128)(2,1)}, bf16[4,2,256,128]{3,2,1,0:T(8,128)(2,1)}) custom-call(bf16[4,16,256,128]{3,2,1,0:T(8,128)(2,1)} %rest_2_.1), custom_call_target="tpu_custom_call" | custom-call | tf_op jit(solution)/shard_map/sums_and_rows/pallas_call | solution.py:78
  3.8 0.0 copy-start
  3.8 0.0 copy-start.1
  3.9 0.0 copy-start.2
  3.9 0.0 copy-start.3
  3.9 0.0 copy-start.4
  3.9 0.0 copy-start.5
  3.9 4.7 %collective-permute-start.3 = (bf16[1,16,256,128]{3,2,1,0:T(8,128)(2,1)}, bf16[1,16,256,128]{3,2,1,0:T(8,128)(2,1)S(1)}, u32[]{:S(2)}, u32[]{:S(2)}) collective-permute-start(bf16[1,16,256,128]{3,2,1,0:T(8,128)(2,1)} %get-tuple-element.14), channel_id=1, source_target_pairs={{0,4},{4,8},{8,12},{12,16},{16,20},{20,24},{24,28},{28,32},{32,36}... | collective-permute-start | bytes 3145736 | tf_op jit(solution)/shard_map/ppermute | solution.py:334
  8.6 1.3 %collective-permute-start.1 = (bf16[4,2,256,128]{3,2,1,0:T(8,128)(2,1)}, bf16[4,2,256,128]{3,2,1,0:T(8,128)(2,1)S(1)}, u32[]{:S(2)}, u32[]{:S(2)}) collective-permute-start(bf16[4,2,256,128]{3,2,1,0:T(8,128)(2,1)} %get-tuple-element.13), channel_id=1, source_target_pairs={{1,0},{2,1},{3,2},{5,4},{6,5},{7,6},{9,8},{10,9},{11,10},{13,12},{... | collective-permute-start | bytes 1572872 | tf_op jit(solution)/shard_map/ppermute | solution.py:332
  9.9 4.2 %collective-permute-start = (bf16[4,1,256,128]{3,2,1,0:T(8,128)(2,1)}, bf16[4,1,256,128]{3,2,1,0:T(8,128)(2,1)S(1)}, u32[]{:S(2)}, u32[]{:S(2)}) collective-permute-start(bf16[4,1,256,128]{3,2,1,0:T(8,128)(2,1)} %get-tuple-element.12), channel_id=1, source_target_pairs={{0,1},{1,2},{2,3},{4,5},{5,6},{6,7},{8,9},{9,10},{10,11},{12,13},{... | collective-permute-start | bytes 786440 | tf_op jit(solution)/shard_map/ppermute | solution.py:331
  14.1 9.5 %all-to-all-start = ((f32[128,2,128]{2,1,0:T(2,128)}), f32[128,2,128]{2,1,0:T(2,128)S(1)}, u32[]{:S(2)}, u32[]{:S(2)}) async-start(f32[128,2,128]{2,1,0:T(2,128)} %get-tuple-element.10), calls=%async_computation | async-start | bytes 262144 | tf_op jit(solution)/shard_map/all_to_all | solution.py:330
  23.6 0.0 copy-done.6
  23.6 0.1 pad_add_fusion.scalars
  23.7 0.0 collective-permute-done.rest_1_.rest_3_
  23.7 0.0 collective-permute-done.1.rest_2_.rest_4_
  23.8 0.8 %maximum_dynamic-update-slice_fusion = bf16[1,22,256,128]{3,2,1,0:T(8,128)(2,1)} fusion(bf16[1,22,256,128]{3,2,1,0:T(8,128)(2,1)} %get-tuple-element.11, bf16[1,4,256,128]{3,2,1,0:T(8,128)(2,1)S(1)} %bitcast.17, bf16[1,2,256,128]{3,2,1,0:T(8,128)(2,1)S(1)} %slice_bitcast_fusion), kind=kLoop, calls=%fused_computation | loop fusion | flops 786432 | bytes 786432 | tf_op jit(solution)/shard_map/dynamic_update_slice | solution.py:336
  24.6 3.5 %collective-permute-start.2 = (bf16[1,22,256,128]{3,2,1,0:T(8,128)(2,1)}, bf16[1,22,256,128]{3,2,1,0:T(8,128)(2,1)}, u32[]{:S(2)}, u32[]{:S(2)}) collective-permute-start(bf16[1,22,256,128]{3,2,1,0:T(8,128)(2,1)} %maximum_dynamic-update-slice_fusion), channel_id=1, source_target_pairs={{0,4},{4,8},{8,12},{12,16},{16,20},{20,24},{24,28},{28,32},{32,36}... | collective-permute-start | bytes 4325384 | tf_op jit(solution)/shard_map/ppermute | solution.py:337
  28.1 5.4 %all-to-all-done.sums_ref = f32[128,2,128]{2,1,0:T(2,128)S(1)} async-done(((f32[128,2,128]{2,1,0:T(2,128)}), f32[128,2,128]{2,1,0:T(2,128)S(1)}, u32[]{:S(2)}, u32[]{:S(2)}) %all-to-all-start) | async-done | bytes 131104 | tf_op jit(solution)/shard_map/all_to_all | solution.py:330
  33.5 0.0 collective-permute-done.3.rest_3_.rest_1_
  33.5 0.0 copy-done
  33.5 0.0 copy-done.1
  33.5 0.0 copy-done.2
  33.5 0.0 copy-done.3
  33.5 0.0 copy-done.4
  33.5 0.0 copy-done.5
  33.6 13.2 %two_frames.2.rest_5_ = bf16[4,8,128,128]{3,2,1,0:T(8,128)(2,1)} custom-call(s32[19]{0:T(128)S(1)} %pad_add_fusion.scalars, f32[1,128]{1,0:T(1,128)S(1)} %bitcast.9, f32[1,128]{1,0:T(1,128)S(1)} %bitcast.11, f32[1,128]{1,0:T(1,128)S(1)} %bitcast.13, f32[1,128]{1,0:T(1,128)S(1)} %bitcast.15, f32[128,2,128]{2,1,0:T(2,128)S(1)} %all-to-all-done.sums_ref, ...), custom_call_target="tpu_custom_call" | custom-call | flops 199999995904 | bytes 6291456 | tf_op jit(solution)/shard_map/two_frames/pallas_call | solution.py:311
  46.8 0.0 collective-permute-done.2.rest_0_
  46.8 13.5 %two_frames.3 = bf16[4,8,128,128]{3,2,1,0:T(8,128)(2,1)} custom-call(s32[19]{0:T(128)S(1)} %pad_add_fusion.scalars, f32[1,128]{1,0:T(1,128)S(1)} %bitcast.10, f32[1,128]{1,0:T(1,128)S(1)} %bitcast.12, f32[1,128]{1,0:T(1,128)S(1)} %bitcast.14, f32[1,128]{1,0:T(1,128)S(1)} %bitcast.16, ...), custom_call_target="tpu_custom_call", output_to_operand_aliasing={{}: (13, {})} | custom-call | flops 199999995904 | bytes 6291456 | tf_op jit(solution)/shard_map/two_frames/pallas_call | solution.py:311
  (2 shorter events, 0.0 us)
Async XLA Ops:
  0.0 23.6 %copy-start.6 = (s32[16]{0:T(128)S(1)}, s32[16]{0:T(128)}, u32[]{:S(2)}) copy-start(s32[16]{0:T(128)} %param.9) | copy-start | bytes 196
  3.8 29.7 %copy-start = (bf16[3,3,3,128,128]{4,3,2,1,0:T(8,128)(2,1)S(1)}, bf16[3,3,3,128,128]{4,3,2,1,0:T(8,128)(2,1)}, u32[]{:S(2)}) copy-start(bf16[3,3,3,128,128]{4,3,2,1,0:T(8,128)(2,1)} %w_ref.3) | copy-start | bytes 2654212
  3.8 29.7 %copy-start.1 = (bf16[3,3,128,128]{3,2,1,0:T(8,128)(2,1)S(1)}, bf16[3,3,128,128]{3,2,1,0:T(8,128)(2,1)}, u32[]{:S(2)}) copy-start(bf16[3,3,128,128]{3,2,1,0:T(8,128)(2,1)} %dw_ref.3) | copy-start | bytes 884740
  3.9 29.7 %copy-start.2 = (f32[128]{0:T(128)S(1)}, f32[128]{0:T(128)}, u32[]{:S(2)}) copy-start(f32[128]{0:T(128)} %param.10) | copy-start | bytes 1540
  3.9 29.7 %copy-start.3 = (f32[128]{0:T(128)S(1)}, f32[128]{0:T(128)}, u32[]{:S(2)}) copy-start(f32[128]{0:T(128)} %param.11) | copy-start | bytes 1540
  3.9 29.7 %copy-start.4 = (f32[128]{0:T(128)S(1)}, f32[128]{0:T(128)}, u32[]{:S(2)}) copy-start(f32[128]{0:T(128)} %param.13) | copy-start | bytes 1540
  3.9 29.7 %copy-start.5 = (f32[128]{0:T(128)S(1)}, f32[128]{0:T(128)}, u32[]{:S(2)}) copy-start(f32[128]{0:T(128)} %param.15) | copy-start | bytes 1540
  3.9 29.6 %collective-permute-start.3 = (bf16[1,16,256,128]{3,2,1,0:T(8,128)(2,1)}, bf16[1,16,256,128]{3,2,1,0:T(8,128)(2,1)S(1)}, u32[]{:S(2)}, u32[]{:S(2)}) collective-permute-start(bf16[1,16,256,128]{3,2,1,0:T(8,128)(2,1)} %get-tuple-element.14), channel_id=1, source_target_pairs={{0,4},{4,8},{8,12},{12,16},{16,20},{20,24},{24,28},{28,32},{32,36}... | collective-permute-start | bytes 3145736 | tf_op jit(solution)/shard_map/ppermute | solution.py:334
  8.6 15.1 %collective-permute-start.1 = (bf16[4,2,256,128]{3,2,1,0:T(8,128)(2,1)}, bf16[4,2,256,128]{3,2,1,0:T(8,128)(2,1)S(1)}, u32[]{:S(2)}, u32[]{:S(2)}) collective-permute-start(bf16[4,2,256,128]{3,2,1,0:T(8,128)(2,1)} %get-tuple-element.13), channel_id=1, source_target_pairs={{1,0},{2,1},{3,2},{5,4},{6,5},{7,6},{9,8},{10,9},{11,10},{13,12},{... | collective-permute-start | bytes 1572872 | tf_op jit(solution)/shard_map/ppermute | solution.py:332
  9.9 13.8 %collective-permute-start = (bf16[4,1,256,128]{3,2,1,0:T(8,128)(2,1)}, bf16[4,1,256,128]{3,2,1,0:T(8,128)(2,1)S(1)}, u32[]{:S(2)}, u32[]{:S(2)}) collective-permute-start(bf16[4,1,256,128]{3,2,1,0:T(8,128)(2,1)} %get-tuple-element.12), channel_id=1, source_target_pairs={{0,1},{1,2},{2,3},{4,5},{5,6},{6,7},{8,9},{9,10},{10,11},{12,13},{... | collective-permute-start | bytes 786440 | tf_op jit(solution)/shard_map/ppermute | solution.py:331
  14.1 19.4 %all-to-all-start = ((f32[128,2,128]{2,1,0:T(2,128)}), f32[128,2,128]{2,1,0:T(2,128)S(1)}, u32[]{:S(2)}, u32[]{:S(2)}) async-start(f32[128,2,128]{2,1,0:T(2,128)} %get-tuple-element.10), calls=%async_computation | async-start | bytes 262144 | tf_op jit(solution)/shard_map/all_to_all | solution.py:330
  24.6 22.2 %collective-permute-start.2 = (bf16[1,22,256,128]{3,2,1,0:T(8,128)(2,1)}, bf16[1,22,256,128]{3,2,1,0:T(8,128)(2,1)}, u32[]{:S(2)}, u32[]{:S(2)}) collective-permute-start(bf16[1,22,256,128]{3,2,1,0:T(8,128)(2,1)} %maximum_dynamic-update-slice_fusion), channel_id=1, source_target_pairs={{0,4},{4,8},{8,12},{12,16},{16,20},{20,24},{24,28},{28,32},{32,36}... | collective-permute-start | bytes 4325384 | tf_op jit(solution)/shard_map/ppermute | solution.py:337

commit v4 on v3

--- a/solution.py
+++ b/solution.py
@@ -272,10 +272,9 @@
     build_weights()
     arrive(0)
     act_step(0)
+    arrive(1)
     for s in range(9):
         conv_step(s)
-        if s == 0:
-            arrive(1)
         if s < 8:
             act_step(s + 1)
     for r in range(8):

time: 60.7 us -> 61.6 us (1.015)
  Pallas kernels: 30.6 us -> 31.4 us
    pallas_call x2, Pallas kernels: 26.7 us -> 27.6 us  [two_frames(): pl.pallas_call(functools.partial(block_kernel, base, target, (len(big) +...]
where the time goes in v4:
time: 61.6 us; the launch traced here: 61.3 us
  Pallas kernels  31.4 us (51%)
  starting transfers between devices  23.2 us (38%)
  waiting for transfers between devices  5.4 us (9%)
  other arithmetic  0.86 us (1%)
    pallas_call x2, Pallas kernels, two_frames(): pl.pallas_call(functools.partial(block_kernel, base, target, (len(big) +...  27.6 us
    all_to_all x1, starting transfers between devices, shards(): sums = lax.all_to_all(sums, both, 0, 0)  9.49 us
    all_to_all x1, waiting for transfers between devices, shards(): sums = lax.all_to_all(sums, both, 0, 0)  5.39 us
    ppermute x1, starting transfers between devices, shards(): near = lax.ppermute(near, 'slab', along)  4.73 us
    ppermute x1, starting transfers between devices, shards(): top = lax.ppermute(top, 'tile', [(t, t + 1) for t in range(tiles - 1)])  4.18 us
    pallas_call x1, Pallas kernels, sums_and_rows(): pl.pallas_call(functools.partial(sums_kernel, pieces), in_specs=[anywhere...  3.82 us
    ppermute x1, starting transfers between devices, shards(): far = lax.ppermute(far, 'slab', along)  3.53 us
    ppermute x1, starting transfers between devices, shards(): lax.ppermute(bottom, 'tile', [(t + 1, t) for t in range(tiles - 1)])  1.29 us
  transfers between devices with their start and end apart: 5, of which 1 were waited for; matrix products, arithmetic and copies ran while one was open for 1% of the time, Pallas kernels for 22%

profile of v4, /device:TPU:1, one launch (start us, length us, event | category | flops | bytes accessed | tf_op | source)
XLA Modules:
  0.0 61.3 jit_solution(11711830778489375392)
XLA Ops:
  0.0 0.0 copy-start.6
  0.0 3.8 %sums_and_rows.1 = (f32[128,2,128]{2,1,0:T(2,128)}, bf16[1,22,256,128]{3,2,1,0:T(8,128)(2,1)}, bf16[1,16,256,128]{3,2,1,0:T(8,128)(2,1)}, bf16[4,1,256,128]{3,2,1,0:T(8,128)(2,1)}, bf16[4,2,256,128]{3,2,1,0:T(8,128)(2,1)}) custom-call(bf16[4,16,256,128]{3,2,1,0:T(8,128)(2,1)} %rest_2_.1), custom_call_target="tpu_custom_call" | custom-call | tf_op jit(solution)/shard_map/sums_and_rows/pallas_call | solution.py:78
  3.8 0.0 copy-start
  3.8 0.0 copy-start.1
  3.9 0.0 copy-start.2
  3.9 0.0 copy-start.3
  3.9 0.0 copy-start.4
  3.9 0.0 copy-start.5
  3.9 4.7 %collective-permute-start.3 = (bf16[1,16,256,128]{3,2,1,0:T(8,128)(2,1)}, bf16[1,16,256,128]{3,2,1,0:T(8,128)(2,1)S(1)}, u32[]{:S(2)}, u32[]{:S(2)}) collective-permute-start(bf16[1,16,256,128]{3,2,1,0:T(8,128)(2,1)} %get-tuple-element.14), channel_id=1, source_target_pairs={{0,4},{4,8},{8,12},{12,16},{16,20},{20,24},{24,28},{28,32},{32,36}... | collective-permute-start | bytes 3145736 | tf_op jit(solution)/shard_map/ppermute | solution.py:333
  8.6 1.3 %collective-permute-start.1 = (bf16[4,2,256,128]{3,2,1,0:T(8,128)(2,1)}, bf16[4,2,256,128]{3,2,1,0:T(8,128)(2,1)S(1)}, u32[]{:S(2)}, u32[]{:S(2)}) collective-permute-start(bf16[4,2,256,128]{3,2,1,0:T(8,128)(2,1)} %get-tuple-element.13), channel_id=1, source_target_pairs={{1,0},{2,1},{3,2},{5,4},{6,5},{7,6},{9,8},{10,9},{11,10},{13,12},{... | collective-permute-start | bytes 1572872 | tf_op jit(solution)/shard_map/ppermute | solution.py:331
  9.9 4.2 %collective-permute-start = (bf16[4,1,256,128]{3,2,1,0:T(8,128)(2,1)}, bf16[4,1,256,128]{3,2,1,0:T(8,128)(2,1)S(1)}, u32[]{:S(2)}, u32[]{:S(2)}) collective-permute-start(bf16[4,1,256,128]{3,2,1,0:T(8,128)(2,1)} %get-tuple-element.12), channel_id=1, source_target_pairs={{0,1},{1,2},{2,3},{4,5},{5,6},{6,7},{8,9},{9,10},{10,11},{12,13},{... | collective-permute-start | bytes 786440 | tf_op jit(solution)/shard_map/ppermute | solution.py:330
  14.1 9.5 %all-to-all-start = ((f32[128,2,128]{2,1,0:T(2,128)}), f32[128,2,128]{2,1,0:T(2,128)S(1)}, u32[]{:S(2)}, u32[]{:S(2)}) async-start(f32[128,2,128]{2,1,0:T(2,128)} %get-tuple-element.10), calls=%async_computation | async-start | bytes 262144 | tf_op jit(solution)/shard_map/all_to_all | solution.py:329
  23.6 0.0 copy-done.6
  23.6 0.1 pad_add_fusion.scalars
  23.7 0.0 collective-permute-done.rest_1_.rest_3_
  23.7 0.0 collective-permute-done.1.rest_2_.rest_4_
  23.8 0.8 %maximum_dynamic-update-slice_fusion = bf16[1,22,256,128]{3,2,1,0:T(8,128)(2,1)} fusion(bf16[1,22,256,128]{3,2,1,0:T(8,128)(2,1)} %get-tuple-element.11, bf16[1,4,256,128]{3,2,1,0:T(8,128)(2,1)S(1)} %bitcast.17, bf16[1,2,256,128]{3,2,1,0:T(8,128)(2,1)S(1)} %slice_bitcast_fusion), kind=kLoop, calls=%fused_computation | loop fusion | flops 786432 | bytes 786432 | tf_op jit(solution)/shard_map/dynamic_update_slice | solution.py:335
  24.6 3.5 %collective-permute-start.2 = (bf16[1,22,256,128]{3,2,1,0:T(8,128)(2,1)}, bf16[1,22,256,128]{3,2,1,0:T(8,128)(2,1)}, u32[]{:S(2)}, u32[]{:S(2)}) collective-permute-start(bf16[1,22,256,128]{3,2,1,0:T(8,128)(2,1)} %maximum_dynamic-update-slice_fusion), channel_id=1, source_target_pairs={{0,4},{4,8},{8,12},{12,16},{16,20},{20,24},{24,28},{28,32},{32,36}... | collective-permute-start | bytes 4325384 | tf_op jit(solution)/shard_map/ppermute | solution.py:336
  28.1 5.4 %all-to-all-done.sums_ref = f32[128,2,128]{2,1,0:T(2,128)S(1)} async-done(((f32[128,2,128]{2,1,0:T(2,128)}), f32[128,2,128]{2,1,0:T(2,128)S(1)}, u32[]{:S(2)}, u32[]{:S(2)}) %all-to-all-start) | async-done | bytes 131104 | tf_op jit(solution)/shard_map/all_to_all | solution.py:329
  33.5 0.0 collective-permute-done.3.rest_3_.rest_1_
  33.5 0.0 copy-done
  33.5 0.0 copy-done.1
  33.5 0.0 copy-done.2
  33.5 0.0 copy-done.3
  33.5 0.0 copy-done.4
  33.5 0.0 copy-done.5
  33.6 13.7 %two_frames.2.rest_5_ = bf16[4,8,128,128]{3,2,1,0:T(8,128)(2,1)} custom-call(s32[19]{0:T(128)S(1)} %pad_add_fusion.scalars, f32[1,128]{1,0:T(1,128)S(1)} %bitcast.9, f32[1,128]{1,0:T(1,128)S(1)} %bitcast.11, f32[1,128]{1,0:T(1,128)S(1)} %bitcast.13, f32[1,128]{1,0:T(1,128)S(1)} %bitcast.15, f32[128,2,128]{2,1,0:T(2,128)S(1)} %all-to-all-done.sums_ref, ...), custom_call_target="tpu_custom_call" | custom-call | flops 199999995904 | bytes 6291456 | tf_op jit(solution)/shard_map/two_frames/pallas_call | solution.py:310
  47.3 0.0 collective-permute-done.2.rest_0_
  47.3 13.8 %two_frames.3 = bf16[4,8,128,128]{3,2,1,0:T(8,128)(2,1)} custom-call(s32[19]{0:T(128)S(1)} %pad_add_fusion.scalars, f32[1,128]{1,0:T(1,128)S(1)} %bitcast.10, f32[1,128]{1,0:T(1,128)S(1)} %bitcast.12, f32[1,128]{1,0:T(1,128)S(1)} %bitcast.14, f32[1,128]{1,0:T(1,128)S(1)} %bitcast.16, ...), custom_call_target="tpu_custom_call", output_to_operand_aliasing={{}: (13, {})} | custom-call | flops 199999995904 | bytes 6291456 | tf_op jit(solution)/shard_map/two_frames/pallas_call | solution.py:310
  (2 shorter events, 0.0 us)
Async XLA Ops:
  0.0 23.6 %copy-start.6 = (s32[16]{0:T(128)S(1)}, s32[16]{0:T(128)}, u32[]{:S(2)}) copy-start(s32[16]{0:T(128)} %param.9) | copy-start | bytes 196
  3.8 29.7 %copy-start = (bf16[3,3,3,128,128]{4,3,2,1,0:T(8,128)(2,1)S(1)}, bf16[3,3,3,128,128]{4,3,2,1,0:T(8,128)(2,1)}, u32[]{:S(2)}) copy-start(bf16[3,3,3,128,128]{4,3,2,1,0:T(8,128)(2,1)} %w_ref.3) | copy-start | bytes 2654212
  3.8 29.7 %copy-start.1 = (bf16[3,3,128,128]{3,2,1,0:T(8,128)(2,1)S(1)}, bf16[3,3,128,128]{3,2,1,0:T(8,128)(2,1)}, u32[]{:S(2)}) copy-start(bf16[3,3,128,128]{3,2,1,0:T(8,128)(2,1)} %dw_ref.3) | copy-start | bytes 884740
  3.9 29.7 %copy-start.2 = (f32[128]{0:T(128)S(1)}, f32[128]{0:T(128)}, u32[]{:S(2)}) copy-start(f32[128]{0:T(128)} %param.10) | copy-start | bytes 1540
  3.9 29.7 %copy-start.3 = (f32[128]{0:T(128)S(1)}, f32[128]{0:T(128)}, u32[]{:S(2)}) copy-start(f32[128]{0:T(128)} %param.11) | copy-start | bytes 1540
  3.9 29.7 %copy-start.4 = (f32[128]{0:T(128)S(1)}, f32[128]{0:T(128)}, u32[]{:S(2)}) copy-start(f32[128]{0:T(128)} %param.13) | copy-start | bytes 1540
  3.9 29.7 %copy-start.5 = (f32[128]{0:T(128)S(1)}, f32[128]{0:T(128)}, u32[]{:S(2)}) copy-start(f32[128]{0:T(128)} %param.15) | copy-start | bytes 1540
  3.9 29.6 %collective-permute-start.3 = (bf16[1,16,256,128]{3,2,1,0:T(8,128)(2,1)}, bf16[1,16,256,128]{3,2,1,0:T(8,128)(2,1)S(1)}, u32[]{:S(2)}, u32[]{:S(2)}) collective-permute-start(bf16[1,16,256,128]{3,2,1,0:T(8,128)(2,1)} %get-tuple-element.14), channel_id=1, source_target_pairs={{0,4},{4,8},{8,12},{12,16},{16,20},{20,24},{24,28},{28,32},{32,36}... | collective-permute-start | bytes 3145736 | tf_op jit(solution)/shard_map/ppermute | solution.py:333
  8.6 15.1 %collective-permute-start.1 = (bf16[4,2,256,128]{3,2,1,0:T(8,128)(2,1)}, bf16[4,2,256,128]{3,2,1,0:T(8,128)(2,1)S(1)}, u32[]{:S(2)}, u32[]{:S(2)}) collective-permute-start(bf16[4,2,256,128]{3,2,1,0:T(8,128)(2,1)} %get-tuple-element.13), channel_id=1, source_target_pairs={{1,0},{2,1},{3,2},{5,4},{6,5},{7,6},{9,8},{10,9},{11,10},{13,12},{... | collective-permute-start | bytes 1572872 | tf_op jit(solution)/shard_map/ppermute | solution.py:331
  9.9 13.8 %collective-permute-start = (bf16[4,1,256,128]{3,2,1,0:T(8,128)(2,1)}, bf16[4,1,256,128]{3,2,1,0:T(8,128)(2,1)S(1)}, u32[]{:S(2)}, u32[]{:S(2)}) collective-permute-start(bf16[4,1,256,128]{3,2,1,0:T(8,128)(2,1)} %get-tuple-element.12), channel_id=1, source_target_pairs={{0,1},{1,2},{2,3},{4,5},{5,6},{6,7},{8,9},{9,10},{10,11},{12,13},{... | collective-permute-start | bytes 786440 | tf_op jit(solution)/shard_map/ppermute | solution.py:330
  14.1 19.4 %all-to-all-start = ((f32[128,2,128]{2,1,0:T(2,128)}), f32[128,2,128]{2,1,0:T(2,128)S(1)}, u32[]{:S(2)}, u32[]{:S(2)}) async-start(f32[128,2,128]{2,1,0:T(2,128)} %get-tuple-element.10), calls=%async_computation | async-start | bytes 262144 | tf_op jit(solution)/shard_map/all_to_all | solution.py:329
  24.6 22.7 %collective-permute-start.2 = (bf16[1,22,256,128]{3,2,1,0:T(8,128)(2,1)}, bf16[1,22,256,128]{3,2,1,0:T(8,128)(2,1)}, u32[]{:S(2)}, u32[]{:S(2)}) collective-permute-start(bf16[1,22,256,128]{3,2,1,0:T(8,128)(2,1)} %maximum_dynamic-update-slice_fusion), channel_id=1, source_target_pairs={{0,4},{4,8},{8,12},{12,16},{16,20},{20,24},{24,28},{28,32},{32,36}... | collective-permute-start | bytes 4325384 | tf_op jit(solution)/shard_map/ppermute | solution.py:336
